TPU v7x, 256 devices: a whole 4x4x8 slice. The times are simulated.
256 devices in a mesh: row: 16 (over x, y_hi, core), col: 16 (over z, y_lo).
Axes of the slice: x: 4, y: 4 (y_hi: 2, y_lo: 2; y = y_hi * 2 + y_lo), z: 8, core: 2. Of those that a mesh axis runs over, the one named last changes fastest.
Arguments:
- block_values: float32 [64, 16, 3, 128, 128], P('row', 'col'), may hold values from -1.5 to 1.5
- block_cols: int32 [64, 16, 3], P('row', 'col'), may hold values from 0 to 3
- result_cols: int32 [64, 16, 4], P('row', 'col'), may hold values from 0 to 3, each once within a row
Outputs:
- square_blocks: float32 [64, 16, 4, 128, 128], P('row', 'col')
Inputs may be any that keep to these rules, and one draw needn't show every extreme that they name: `block_cols`: a stored block's column inside its run of 4 block columns; several stored blocks may share a column. For each block row i and each tile q, result_cols[i, q, :] is a permutation of 0 to 3, so each value appears once in every tile and 16 times over a whole block row.
All inputs are finite; a program needn't handle non-finite values.
Results may differ from a plain program's by a relative error of at most 0.0003.
Values sent between devices are 32-bit elements; how exact they have to be, the bound alone decides.
A program may use at most 192 MiB of HBM per device.

v0:
```python
import jax
import jax.numpy as jnp
from jax import lax
from jax.sharding import PartitionSpec as P


def passed_along(value, axis, steps):
    count = lax.axis_size(axis)
    pairs = [(source, (source + steps) % count) for source in range(count)]
    return lax.ppermute(value, axis, pairs)


def multiply_pieces(left_values, left_cols, right_values, right_cols, local_targets, running):
    left_rows = left_cols.shape[0]
    left_pieces = left_cols.shape[1]
    tile_rows = right_values.shape[0] // left_pieces
    piece_ids = jnp.arange(left_pieces, dtype=jnp.int32)
    inner_rows = (piece_ids[None, :, None] * tile_rows + left_cols).reshape(left_rows, -1)
    left_flat = left_values.reshape(left_rows, -1, left_values.shape[-2], left_values.shape[-1])
    right_pieces = right_cols.shape[1]
    right_ids = jnp.arange(right_pieces, dtype=jnp.int32)
    right_local = (right_ids[None, :, None] * tile_rows + right_cols).reshape(
        right_cols.shape[0], -1
    )
    right_flat = right_values.reshape(
        right_values.shape[0], -1, right_values.shape[-2], right_values.shape[-1]
    )
    chosen_blocks = right_flat[inner_rows]
    chosen_cols = right_local[inner_rows]
    products = jnp.einsum(
        "imxy,imnyz->imnxz", left_flat, chosen_blocks, precision=lax.Precision.HIGHEST
    )
    matches = (chosen_cols[:, :, :, None] == local_targets[:, None, None, :]).astype(jnp.float32)
    return running + jnp.einsum(
        "imnu,imnxz->iuxz", matches, products, precision=lax.Precision.HIGHEST
    )


def on_device(block_values, block_cols, result_cols):
    n_rowdev = lax.axis_size("row")
    n_coldev = lax.axis_size("col")
    pieces_dev = n_rowdev // n_coldev
    here_row = lax.axis_index("row")
    here_col = lax.axis_index("col")
    tile_rows = block_values.shape[0]
    order = block_values.shape[-1]
    local_targets = result_cols[:, 0, :]
    running = jnp.zeros((tile_rows, local_targets.shape[1], order, order), jnp.float32)
    levels = (n_rowdev - 1).bit_length()
    queue_values, queue_cols = (block_values, block_cols)
    for level in range(levels):
        amount = 1 << level
        shifted_values, shifted_cols = passed_along(
            (queue_values, queue_cols), "col", -max(amount // pieces_dev, 1)
        )
        chosen_bit = here_row >> level & 1 == 1
        queue_values = jnp.where(chosen_bit, shifted_values, queue_values)
        queue_cols = jnp.where(chosen_bit, shifted_cols, queue_cols)
    rows_values, rows_cols = (block_values, block_cols)
    row_lift = here_col * pieces_dev % n_rowdev
    for level in range(levels):
        shifted_values, shifted_cols = passed_along((rows_values, rows_cols), "row", -(1 << level))
        chosen_bit = row_lift >> level & 1 == 1
        rows_values = jnp.where(chosen_bit, shifted_values, rows_values)
        rows_cols = jnp.where(chosen_bit, shifted_cols, rows_cols)

    def one_step(step_index, carried):
        queue_values, queue_cols, rows_values, rows_cols, running = carried
        running = multiply_pieces(
            queue_values, queue_cols, rows_values, rows_cols, local_targets, running
        )
        head_values, head_cols = passed_along((queue_values, queue_cols), "col", -1)
        queue_values = jnp.concatenate([queue_values[:, 1:], head_values], axis=1)
        queue_cols = jnp.concatenate([queue_cols[:, 1:], head_cols], axis=1)
        rows_values, rows_cols = passed_along((rows_values, rows_cols), "row", -1)
        return (queue_values, queue_cols, rows_values, rows_cols, running)

    queue_values, queue_cols, rows_values, rows_cols, running = lax.fori_loop(
        0, n_rowdev - 1, one_step, (queue_values, queue_cols, rows_values, rows_cols, running)
    )
    running = multiply_pieces(
        queue_values, queue_cols, rows_values, rows_cols, local_targets, running
    )
    return running.reshape(tile_rows, 1, local_targets.shape[1], order, order)


def solution(mesh):
    return jax.shard_map(
        on_device,
        mesh=mesh,
        in_specs=(P("row", "col", None, None, None), P("row", "col", None), P("row", "col", None)),
        out_specs=P("row", "col", None, None, None),
        check_vma=False,
    )
```

profile of v0, /device:TPU:1, one launch (start us, length us, event | category | flops | bytes accessed | tf_op | source)
XLA Modules:
  0.0 695.8 jit_solution(13392830147680571129)
XLA Ops:
  8.1 22.9 %collective-permute-done.12 = f32[4,1,3,128,128]{4,3,2,1,0:T(8,128)S(1)} collective-permute-done((f32[4,1,3,128,128]{4,3,2,1,0:T(8,128)}, f32[4,1,3,128,128]{4,3,2,1,0:T(8,128)S(1)}, u32[]{:S(2)}, u32[]{:S(2)}) %collective-permute-start.12) | collective-permute-done | bytes 786464 | tf_op jit(solution)/shard_map/ppermute | solution.py:10
  42.8 10.7 %collective-permute-done.16 = s32[4,1,3]{2,0,1:T(4,128)S(1)} collective-permute-done((s32[4,1,3]{2,0,1:T(4,128)S(1)}, s32[4,1,3]{2,0,1:T(4,128)S(1)}, u32[]{:S(2)}, u32[]{:S(2)}) %collective-permute-start.16) | collective-permute-done | bytes 80 | tf_op jit(solution)/shard_map/ppermute | solution.py:10
  65.1 15.8 %collective-permute-done.18 = s32[4,1,3]{2,0,1:T(4,128)S(1)} collective-permute-done((s32[4,1,3]{2,0,1:T(4,128)S(1)}, s32[4,1,3]{2,0,1:T(4,128)S(1)}, u32[]{:S(2)}, u32[]{:S(2)}) %collective-permute-start.18) | collective-permute-done | bytes 80 | tf_op jit(solution)/shard_map/ppermute | solution.py:10
  84.1 14.2 %collective-permute-done.6 = f32[4,1,3,128,128]{4,3,2,1,0:T(8,128)S(1)} collective-permute-done((f32[4,1,3,128,128]{4,3,2,1,0:T(8,128)S(1)}, f32[4,1,3,128,128]{4,3,2,1,0:T(8,128)S(1)}, u32[]{:S(2)}, u32[]{:S(2)}) %collective-permute-start.6) | collective-permute-done | bytes 786464 | tf_op jit(solution)/shard_map/ppermute | solution.py:10
  104.1 31.1 %collective-permute-done.11 = s32[4,1,3]{0,1,2:T(1,128)S(1)} collective-permute-done((s32[4,1,3]{0,1,2:T(1,128)S(1)}, s32[4,1,3]{0,1,2:T(1,128)S(1)}, u32[]{:S(2)}, u32[]{:S(2)}) %collective-permute-start.11) | collective-permute-done | bytes 80 | tf_op jit(solution)/shard_map/ppermute | solution.py:10
  137.2 541.5 %while.19 = (s32[]{:T(128)}, f32[4,1,3,128,128]{4,3,2,1,0:T(8,128)}, s32[4,1,3]{0,1,2:T(1,128)S(1)}, f32[4,1,3,128,128]{4,3,2,1,0:T(8,128)}, s32[4,1,3]{2,0,1:T(...) while((s32[]{:T(128)}, ...), condition=%wide.region_1.2_spmd.clone, body=%wide.region_0.1_spmd.clone.sunk | while | flops 934806720 | bytes 28841988 | solution.py:78
  151.3 6.7 fusion.37
  166.2 23.1 %collective-permute-done.3 = s32[4,1,3]{2,0,1:T(4,128)S(1)} collective-permute-done((s32[4,1,3]{2,0,1:T(4,128)S(1)}, s32[4,1,3]{2,0,1:T(4,128)S(1)}, u32[]{:S(2)}, u32[]{:S(2)}) %collective-permute-start.3) | collective-permute-done | bytes 80 | tf_op jit(solution)/shard_map/while/body/eval_jaxpr/ppermute | solution.py:10
  211.5 16.7 %collective-permute-done.3 = s32[4,1,3]{2,0,1:T(4,128)S(1)} collective-permute-done((s32[4,1,3]{2,0,1:T(4,128)S(1)}, s32[4,1,3]{2,0,1:T(4,128)S(1)}, u32[]{:S(2)}, u32[]{:S(2)}) %collective-permute-start.3) | collective-permute-done | bytes 80 | tf_op jit(solution)/shard_map/while/body/eval_jaxpr/ppermute | solution.py:10
  235.1 6.7 fusion.37
  251.0 10.7 %collective-permute-done.3 = s32[4,1,3]{2,0,1:T(4,128)S(1)} collective-permute-done((s32[4,1,3]{2,0,1:T(4,128)S(1)}, s32[4,1,3]{2,0,1:T(4,128)S(1)}, u32[]{:S(2)}, u32[]{:S(2)}) %collective-permute-start.3) | collective-permute-done | bytes 80 | tf_op jit(solution)/shard_map/while/body/eval_jaxpr/ppermute | solution.py:10
  310.6 8.2 %collective-permute-done.3 = s32[4,1,3]{2,0,1:T(4,128)S(1)} collective-permute-done((s32[4,1,3]{2,0,1:T(4,128)S(1)}, s32[4,1,3]{2,0,1:T(4,128)S(1)}, u32[]{:S(2)}, u32[]{:S(2)}) %collective-permute-start.3) | collective-permute-done | bytes 80 | tf_op jit(solution)/shard_map/while/body/eval_jaxpr/ppermute | solution.py:10
  323.0 12.3 %collective-permute-start.1 = (s32[4,1,3]{0,1,2:T(1,128)S(1)}, s32[4,1,3]{0,1,2:T(1,128)S(1)}, u32[]{:S(2)}, u32[]{:S(2)}) collective-permute-start(s32[4,1,3]{0,1,2:T(1,128)S(1)} %copy.46), channel_id=1, source_target_pairs={{0,15},{1,0},{2,1},{3,2},{4,3},{5,4},{6,5},{7,6},{8,7},{9,8},{10,9... | collective-permute-start | bytes 152 | tf_op jit(solution)/shard_map/while/body/eval_jaxpr/ppermute | solution.py:10
  355.3 11.0 %collective-permute-start = (f32[4,1,3,128,128]{4,3,2,1,0:T(8,128)}, f32[4,1,3,128,128]{4,3,2,1,0:T(8,128)}, u32[]{:S(2)}, u32[]{:S(2)}) collective-permute-start(f32[4,1,3,128,128]{4,3,2,1,0:T(8,128)} %copy.45), channel_id=1, source_target_pairs={{0,15},{1,0},{2,1},{3,2},{4,3},{5,4},{6,5},{7,6},{8,7},{9,8},{10,9... | collective-permute-start | bytes 2359304 | tf_op jit(solution)/shard_map/while/body/eval_jaxpr/ppermute | solution.py:10
  388.5 9.7 %collective-permute-start = (f32[4,1,3,128,128]{4,3,2,1,0:T(8,128)}, f32[4,1,3,128,128]{4,3,2,1,0:T(8,128)}, u32[]{:S(2)}, u32[]{:S(2)}) collective-permute-start(f32[4,1,3,128,128]{4,3,2,1,0:T(8,128)} %copy.45), channel_id=1, source_target_pairs={{0,15},{1,0},{2,1},{3,2},{4,3},{5,4},{6,5},{7,6},{8,7},{9,8},{10,9... | collective-permute-start | bytes 2359304 | tf_op jit(solution)/shard_map/while/body/eval_jaxpr/ppermute | solution.py:10
  400.4 20.5 %collective-permute-start.1 = (s32[4,1,3]{0,1,2:T(1,128)S(1)}, s32[4,1,3]{0,1,2:T(1,128)S(1)}, u32[]{:S(2)}, u32[]{:S(2)}) collective-permute-start(s32[4,1,3]{0,1,2:T(1,128)S(1)} %copy.46), channel_id=1, source_target_pairs={{0,15},{1,0},{2,1},{3,2},{4,3},{5,4},{6,5},{7,6},{8,7},{9,8},{10,9... | collective-permute-start | bytes 152 | tf_op jit(solution)/shard_map/while/body/eval_jaxpr/ppermute | solution.py:10
  422.9 6.7 fusion.37
  445.9 6.7 fusion.37
  464.4 8.5 %collective-permute-start = (f32[4,1,3,128,128]{4,3,2,1,0:T(8,128)}, f32[4,1,3,128,128]{4,3,2,1,0:T(8,128)}, u32[]{:S(2)}, u32[]{:S(2)}) collective-permute-start(f32[4,1,3,128,128]{4,3,2,1,0:T(8,128)} %copy.45), channel_id=1, source_target_pairs={{0,15},{1,0},{2,1},{3,2},{4,3},{5,4},{6,5},{7,6},{8,7},{9,8},{10,9... | collective-permute-start | bytes 2359304 | tf_op jit(solution)/shard_map/while/body/eval_jaxpr/ppermute | solution.py:10
  475.0 20.7 %collective-permute-start.1 = (s32[4,1,3]{0,1,2:T(1,128)S(1)}, s32[4,1,3]{0,1,2:T(1,128)S(1)}, u32[]{:S(2)}, u32[]{:S(2)}) collective-permute-start(s32[4,1,3]{0,1,2:T(1,128)S(1)} %copy.46), channel_id=1, source_target_pairs={{0,15},{1,0},{2,1},{3,2},{4,3},{5,4},{6,5},{7,6},{8,7},{9,8},{10,9... | collective-permute-start | bytes 152 | tf_op jit(solution)/shard_map/while/body/eval_jaxpr/ppermute | solution.py:10
  539.2 8.5 %collective-permute-start = (f32[4,1,3,128,128]{4,3,2,1,0:T(8,128)}, f32[4,1,3,128,128]{4,3,2,1,0:T(8,128)}, u32[]{:S(2)}, u32[]{:S(2)}) collective-permute-start(f32[4,1,3,128,128]{4,3,2,1,0:T(8,128)} %copy.45), channel_id=1, source_target_pairs={{0,15},{1,0},{2,1},{3,2},{4,3},{5,4},{6,5},{7,6},{8,7},{9,8},{10,9... | collective-permute-start | bytes 2359304 | tf_op jit(solution)/shard_map/while/body/eval_jaxpr/ppermute | solution.py:10
  549.8 20.4 %collective-permute-start.1 = (s32[4,1,3]{0,1,2:T(1,128)S(1)}, s32[4,1,3]{0,1,2:T(1,128)S(1)}, u32[]{:S(2)}, u32[]{:S(2)}) collective-permute-start(s32[4,1,3]{0,1,2:T(1,128)S(1)} %copy.46), channel_id=1, source_target_pairs={{0,15},{1,0},{2,1},{3,2},{4,3},{5,4},{6,5},{7,6},{8,7},{9,8},{10,9... | collective-permute-start | bytes 152 | tf_op jit(solution)/shard_map/while/body/eval_jaxpr/ppermute | solution.py:10
  613.7 8.5 %collective-permute-start = (f32[4,1,3,128,128]{4,3,2,1,0:T(8,128)}, f32[4,1,3,128,128]{4,3,2,1,0:T(8,128)}, u32[]{:S(2)}, u32[]{:S(2)}) collective-permute-start(f32[4,1,3,128,128]{4,3,2,1,0:T(8,128)} %copy.45), channel_id=1, source_target_pairs={{0,15},{1,0},{2,1},{3,2},{4,3},{5,4},{6,5},{7,6},{8,7},{9,8},{10,9... | collective-permute-start | bytes 2359304 | tf_op jit(solution)/shard_map/while/body/eval_jaxpr/ppermute | solution.py:10
  656.8 6.7 fusion.37
  (374 shorter events, 387.6 us)
Async XLA Ops:
  62.8 35.5 %collective-permute-start.6 = (f32[4,1,3,128,128]{4,3,2,1,0:T(8,128)S(1)}, f32[4,1,3,128,128]{4,3,2,1,0:T(8,128)S(1)}, u32[]{:S(2)}, u32[]{:S(2)}) collective-permute-start(f32[4,1,3,128,128]{4,3,2,1,0:T(8,128)S(1)} %broadcast_select_fusion.5), channel_id=1, source_target_pairs={{0,12},{1,13},{2,14},{3,15},{4,0},{5,1},{6,2},{7,3},{8,4},{9,5},{1... | collective-permute-start | bytes 2359304 | tf_op jit(solution)/shard_map/ppermute | solution.py:10
  64.6 36.7 %collective-permute-start.10 = (s32[4,1,3]{0,1,2:T(1,128)S(1)}, s32[4,1,3]{0,1,2:T(1,128)S(1)}, u32[]{:S(2)}, u32[]{:S(2)}) collective-permute-start(s32[4,1,3]{0,1,2:T(1,128)S(1)} %broadcast_select_fusion.9), channel_id=1, source_target_pairs={{0,12},{1,13},{2,14},{3,15},{4,0},{5,1},{6,2},{7,3},{8,4},{9,5},{1... | collective-permute-start | bytes 152 | tf_op jit(solution)/shard_map/ppermute | solution.py:10
  80.9 54.3 %collective-permute-start.19 = (s32[4,1,3]{2,0,1:T(4,128)S(1)}, s32[4,1,3]{2,0,1:T(4,128)S(1)}, u32[]{:S(2)}, u32[]{:S(2)}) collective-permute-start(s32[4,1,3]{2,0,1:T(4,128)S(1)} %broadcast_select_fusion.14), channel_id=1, source_target_pairs={{0,128},{16,144},{32,160},{48,176},{64,192},{80,208},{96,224},{112... | collective-permute-start | bytes 152 | tf_op jit(solution)/shard_map/ppermute | solution.py:10
  81.6 53.7 %collective-permute-start.15 = (f32[4,1,3,128,128]{4,3,2,1,0:T(8,128)S(1)}, f32[4,1,3,128,128]{4,3,2,1,0:T(8,128)S(1)}, u32[]{:S(2)}, u32[]{:S(2)}) collective-permute-start(f32[4,1,3,128,128]{4,3,2,1,0:T(8,128)S(1)} %broadcast_select_fusion.2), channel_id=1, source_target_pairs={{0,128},{16,144},{32,160},{48,176},{64,192},{80,208},{96,224},{112... | collective-permute-start | bytes 2359304 | tf_op jit(solution)/shard_map/ppermute | solution.py:10
  98.4 37.9 %collective-permute-start.7 = (f32[4,1,3,128,128]{4,3,2,1,0:T(8,128)S(1)}, f32[4,1,3,128,128]{4,3,2,1,0:T(8,128)S(1)}, u32[]{:S(2)}, u32[]{:S(2)}) collective-permute-start(f32[4,1,3,128,128]{4,3,2,1,0:T(8,128)S(1)} %broadcast_select_fusion.6), channel_id=1, source_target_pairs={{0,8},{1,9},{2,10},{3,11},{4,12},{5,13},{6,14},{7,15},{8,0},{9,1},... | collective-permute-start | bytes 2359304 | tf_op jit(solution)/shard_map/ppermute | solution.py:10
  139.3 49.9 %collective-permute-start = (f32[4,1,3,128,128]{4,3,2,1,0:T(8,128)}, f32[4,1,3,128,128]{4,3,2,1,0:T(8,128)}, u32[]{:S(2)}, u32[]{:S(2)}) collective-permute-start(f32[4,1,3,128,128]{4,3,2,1,0:T(8,128)} %copy.45), channel_id=1, source_target_pairs={{0,15},{1,0},{2,1},{3,2},{4,3},{5,4},{6,5},{7,6},{8,7},{9,8},{10,9... | collective-permute-start | bytes 2359304 | tf_op jit(solution)/shard_map/while/body/eval_jaxpr/ppermute | solution.py:10
  141.4 47.9 %collective-permute-start.2 = (f32[4,1,3,128,128]{4,3,2,1,0:T(8,128)}, f32[4,1,3,128,128]{4,3,2,1,0:T(8,128)}, u32[]{:S(2)}, u32[]{:S(2)}) collective-permute-start(f32[4,1,3,128,128]{4,3,2,1,0:T(8,128)} %copy.47), channel_id=1, source_target_pairs={{0,240},{16,0},{32,16},{48,32},{64,48},{80,64},{96,80},{112,96},{1... | collective-permute-start | bytes 2359304 | tf_op jit(solution)/shard_map/while/body/eval_jaxpr/ppermute | solution.py:10
  143.8 45.5 %collective-permute-start.3 = (s32[4,1,3]{2,0,1:T(4,128)S(1)}, s32[4,1,3]{2,0,1:T(4,128)S(1)}, u32[]{:S(2)}, u32[]{:S(2)}) collective-permute-start(s32[4,1,3]{2,0,1:T(4,128)S(1)} %copy.48), channel_id=1, source_target_pairs={{0,240},{16,0},{32,16},{48,32},{64,48},{80,64},{96,80},{112,96},{1... | collective-permute-start | bytes 152 | tf_op jit(solution)/shard_map/while/body/eval_jaxpr/ppermute | solution.py:10
  148.0 41.3 %collective-permute-start.1 = (s32[4,1,3]{0,1,2:T(1,128)S(1)}, s32[4,1,3]{0,1,2:T(1,128)S(1)}, u32[]{:S(2)}, u32[]{:S(2)}) collective-permute-start(s32[4,1,3]{0,1,2:T(1,128)S(1)} %copy.46), channel_id=1, source_target_pairs={{0,15},{1,0},{2,1},{3,2},{4,3},{5,4},{6,5},{7,6},{8,7},{9,8},{10,9... | collective-permute-start | bytes 152 | tf_op jit(solution)/shard_map/while/body/eval_jaxpr/ppermute | solution.py:10
  191.4 36.8 %collective-permute-start = (f32[4,1,3,128,128]{4,3,2,1,0:T(8,128)}, f32[4,1,3,128,128]{4,3,2,1,0:T(8,128)}, u32[]{:S(2)}, u32[]{:S(2)}) collective-permute-start(f32[4,1,3,128,128]{4,3,2,1,0:T(8,128)} %copy.45), channel_id=1, source_target_pairs={{0,15},{1,0},{2,1},{3,2},{4,3},{5,4},{6,5},{7,6},{8,7},{9,8},{10,9... | collective-permute-start | bytes 2359304 | tf_op jit(solution)/shard_map/while/body/eval_jaxpr/ppermute | solution.py:10
  193.5 34.7 %collective-permute-start.2 = (f32[4,1,3,128,128]{4,3,2,1,0:T(8,128)}, f32[4,1,3,128,128]{4,3,2,1,0:T(8,128)}, u32[]{:S(2)}, u32[]{:S(2)}) collective-permute-start(f32[4,1,3,128,128]{4,3,2,1,0:T(8,128)} %copy.47), channel_id=1, source_target_pairs={{0,240},{16,0},{32,16},{48,32},{64,48},{80,64},{96,80},{112,96},{1... | collective-permute-start | bytes 2359304 | tf_op jit(solution)/shard_map/while/body/eval_jaxpr/ppermute | solution.py:10
  388.5 50.3 %collective-permute-start = (f32[4,1,3,128,128]{4,3,2,1,0:T(8,128)}, f32[4,1,3,128,128]{4,3,2,1,0:T(8,128)}, u32[]{:S(2)}, u32[]{:S(2)}) collective-permute-start(f32[4,1,3,128,128]{4,3,2,1,0:T(8,128)} %copy.45), channel_id=1, source_target_pairs={{0,15},{1,0},{2,1},{3,2},{4,3},{5,4},{6,5},{7,6},{8,7},{9,8},{10,9... | collective-permute-start | bytes 2359304 | tf_op jit(solution)/shard_map/while/body/eval_jaxpr/ppermute | solution.py:10
  400.3 38.5 %collective-permute-start.2 = (f32[4,1,3,128,128]{4,3,2,1,0:T(8,128)}, f32[4,1,3,128,128]{4,3,2,1,0:T(8,128)}, u32[]{:S(2)}, u32[]{:S(2)}) collective-permute-start(f32[4,1,3,128,128]{4,3,2,1,0:T(8,128)} %copy.47), channel_id=1, source_target_pairs={{0,240},{16,0},{32,16},{48,32},{64,48},{80,64},{96,80},{112,96},{1... | collective-permute-start | bytes 2359304 | tf_op jit(solution)/shard_map/while/body/eval_jaxpr/ppermute | solution.py:10
  400.3 38.5 %collective-permute-start.3 = (s32[4,1,3]{2,0,1:T(4,128)S(1)}, s32[4,1,3]{2,0,1:T(4,128)S(1)}, u32[]{:S(2)}, u32[]{:S(2)}) collective-permute-start(s32[4,1,3]{2,0,1:T(4,128)S(1)} %copy.48), channel_id=1, source_target_pairs={{0,240},{16,0},{32,16},{48,32},{64,48},{80,64},{96,80},{112,96},{1... | collective-permute-start | bytes 152 | tf_op jit(solution)/shard_map/while/body/eval_jaxpr/ppermute | solution.py:10
  400.4 38.5 %collective-permute-start.1 = (s32[4,1,3]{0,1,2:T(1,128)S(1)}, s32[4,1,3]{0,1,2:T(1,128)S(1)}, u32[]{:S(2)}, u32[]{:S(2)}) collective-permute-start(s32[4,1,3]{0,1,2:T(1,128)S(1)} %copy.46), channel_id=1, source_target_pairs={{0,15},{1,0},{2,1},{3,2},{4,3},{5,4},{6,5},{7,6},{8,7},{9,8},{10,9... | collective-permute-start | bytes 152 | tf_op jit(solution)/shard_map/while/body/eval_jaxpr/ppermute | solution.py:10
  464.4 49.2 %collective-permute-start = (f32[4,1,3,128,128]{4,3,2,1,0:T(8,128)}, f32[4,1,3,128,128]{4,3,2,1,0:T(8,128)}, u32[]{:S(2)}, u32[]{:S(2)}) collective-permute-start(f32[4,1,3,128,128]{4,3,2,1,0:T(8,128)} %copy.45), channel_id=1, source_target_pairs={{0,15},{1,0},{2,1},{3,2},{4,3},{5,4},{6,5},{7,6},{8,7},{9,8},{10,9... | collective-permute-start | bytes 2359304 | tf_op jit(solution)/shard_map/while/body/eval_jaxpr/ppermute | solution.py:10
  474.9 38.7 %collective-permute-start.2 = (f32[4,1,3,128,128]{4,3,2,1,0:T(8,128)}, f32[4,1,3,128,128]{4,3,2,1,0:T(8,128)}, u32[]{:S(2)}, u32[]{:S(2)}) collective-permute-start(f32[4,1,3,128,128]{4,3,2,1,0:T(8,128)} %copy.47), channel_id=1, source_target_pairs={{0,240},{16,0},{32,16},{48,32},{64,48},{80,64},{96,80},{112,96},{1... | collective-permute-start | bytes 2359304 | tf_op jit(solution)/shard_map/while/body/eval_jaxpr/ppermute | solution.py:10
  474.9 38.7 %collective-permute-start.3 = (s32[4,1,3]{2,0,1:T(4,128)S(1)}, s32[4,1,3]{2,0,1:T(4,128)S(1)}, u32[]{:S(2)}, u32[]{:S(2)}) collective-permute-start(s32[4,1,3]{2,0,1:T(4,128)S(1)} %copy.48), channel_id=1, source_target_pairs={{0,240},{16,0},{32,16},{48,32},{64,48},{80,64},{96,80},{112,96},{1... | collective-permute-start | bytes 152 | tf_op jit(solution)/shard_map/while/body/eval_jaxpr/ppermute | solution.py:10
  475.0 38.7 %collective-permute-start.1 = (s32[4,1,3]{0,1,2:T(1,128)S(1)}, s32[4,1,3]{0,1,2:T(1,128)S(1)}, u32[]{:S(2)}, u32[]{:S(2)}) collective-permute-start(s32[4,1,3]{0,1,2:T(1,128)S(1)} %copy.46), channel_id=1, source_target_pairs={{0,15},{1,0},{2,1},{3,2},{4,3},{5,4},{6,5},{7,6},{8,7},{9,8},{10,9... | collective-permute-start | bytes 152 | tf_op jit(solution)/shard_map/while/body/eval_jaxpr/ppermute | solution.py:10
  539.2 48.9 %collective-permute-start = (f32[4,1,3,128,128]{4,3,2,1,0:T(8,128)}, f32[4,1,3,128,128]{4,3,2,1,0:T(8,128)}, u32[]{:S(2)}, u32[]{:S(2)}) collective-permute-start(f32[4,1,3,128,128]{4,3,2,1,0:T(8,128)} %copy.45), channel_id=1, source_target_pairs={{0,15},{1,0},{2,1},{3,2},{4,3},{5,4},{6,5},{7,6},{8,7},{9,8},{10,9... | collective-permute-start | bytes 2359304 | tf_op jit(solution)/shard_map/while/body/eval_jaxpr/ppermute | solution.py:10
  549.8 38.4 %collective-permute-start.2 = (f32[4,1,3,128,128]{4,3,2,1,0:T(8,128)}, f32[4,1,3,128,128]{4,3,2,1,0:T(8,128)}, u32[]{:S(2)}, u32[]{:S(2)}) collective-permute-start(f32[4,1,3,128,128]{4,3,2,1,0:T(8,128)} %copy.47), channel_id=1, source_target_pairs={{0,240},{16,0},{32,16},{48,32},{64,48},{80,64},{96,80},{112,96},{1... | collective-permute-start | bytes 2359304 | tf_op jit(solution)/shard_map/while/body/eval_jaxpr/ppermute | solution.py:10
  549.8 38.4 %collective-permute-start.3 = (s32[4,1,3]{2,0,1:T(4,128)S(1)}, s32[4,1,3]{2,0,1:T(4,128)S(1)}, u32[]{:S(2)}, u32[]{:S(2)}) collective-permute-start(s32[4,1,3]{2,0,1:T(4,128)S(1)} %copy.48), channel_id=1, source_target_pairs={{0,240},{16,0},{32,16},{48,32},{64,48},{80,64},{96,80},{112,96},{1... | collective-permute-start | bytes 152 | tf_op jit(solution)/shard_map/while/body/eval_jaxpr/ppermute | solution.py:10
  549.8 38.4 %collective-permute-start.1 = (s32[4,1,3]{0,1,2:T(1,128)S(1)}, s32[4,1,3]{0,1,2:T(1,128)S(1)}, u32[]{:S(2)}, u32[]{:S(2)}) collective-permute-start(s32[4,1,3]{0,1,2:T(1,128)S(1)} %copy.46), channel_id=1, source_target_pairs={{0,15},{1,0},{2,1},{3,2},{4,3},{5,4},{6,5},{7,6},{8,7},{9,8},{10,9... | collective-permute-start | bytes 152 | tf_op jit(solution)/shard_map/while/body/eval_jaxpr/ppermute | solution.py:10
  613.7 34.7 %collective-permute-start = (f32[4,1,3,128,128]{4,3,2,1,0:T(8,128)}, f32[4,1,3,128,128]{4,3,2,1,0:T(8,128)}, u32[]{:S(2)}, u32[]{:S(2)}) collective-permute-start(f32[4,1,3,128,128]{4,3,2,1,0:T(8,128)} %copy.45), channel_id=1, source_target_pairs={{0,15},{1,0},{2,1},{3,2},{4,3},{5,4},{6,5},{7,6},{8,7},{9,8},{10,9... | collective-permute-start | bytes 2359304 | tf_op jit(solution)/shard_map/while/body/eval_jaxpr/ppermute | solution.py:10
  (55 other events, 1284.7 us)
where the time goes:
time: 700 us; the launch traced here: 696 us
  matrix products  191 us (27%)
  starting transfers between devices  173 us (25%)
  waiting for transfers between devices  171 us (24%)
  local copies, waits for them, and re-layouts  155 us (22%)
    ppermute x76, starting transfers between devices, passed_along(): return lax.ppermute(value, axis, pairs)  173 us
    ppermute x76, waiting for transfers between devices, passed_along(): return lax.ppermute(value, axis, pairs)  171 us
    dot_general x16, matrix products, multiply_pieces(): jnp.einsum('imxy,imnyz->imnxz', left_flat, chosen_blocks, precision=lax.P...  107 us
    dot_general x16, matrix products, multiply_pieces(): jnp.einsum('imnu,imnxz->iuxz', matches, products, precision=lax.Precision...  84.2 us
    while x60, local copies, waits for them, and re-layouts  62.3 us
    dot_general x16, local copies, waits for them, and re-layouts, multiply_pieces(): jnp.einsum('imxy,imnyz->imnxz', left_flat, chosen_blocks, precision=lax.P...  50.4 us
    gather x16, local copies, waits for them, and re-layouts, multiply_pieces(): chosen_blocks = right_flat[inner_rows]  29.3 us
  transfers between devices with their start and end apart: 76, of which 16 were waited for; matrix products, arithmetic and copies ran while one was open for 43% of the time, Pallas kernels for 0%

commit v1 on v0

v1 whole, which is shorter than its diff:
```python
import functools

import jax
import jax.numpy as jnp
from jax import lax
from jax.experimental import pallas as pl
from jax.experimental.pallas import tpu as pltpu
from jax.sharding import PartitionSpec as P

MESH = pl.DeviceIdType.MESH
NX, NZ = 4, 8
ORDER = 128
STORED, SLOTS, ROWS = 3, 4, 4
BODY = STORED * ORDER
PIECE = BODY + 8
CUT = 192
RING = 7 * ROWS
STEPS = 35

PRODUCTS = (
    (9, 0, 0, 0),
    (15, 0, 0, 1),
    (16, 1, 0, 0),
    (17, 1, 0, 1),
    (21, 2, 0, 0),
    (22, 2, 0, 1),
    (23, 0, 1, 0),
    (24, 1, 1, 0),
    (25, 2, 1, 0),
    (28, 3, 0, 0),
    (29, 3, 0, 1),
    (30, 0, 1, 1),
    (31, 1, 1, 1),
    (32, 2, 1, 1),
    (33, 3, 1, 0),
    (34, 3, 1, 1),
)


def spread(piece, write):
    step = 32
    heads = [piece[BODY + s : BODY + s + 1, :] for s in range(STORED)]
    hits = [
        [jnp.broadcast_to(heads[s], (step, ORDER)) == float(k) for s in range(STORED)]
        for k in range(SLOTS)
    ]
    for r in range(0, ORDER, step):
        blocks = [piece[s * ORDER + r : s * ORDER + r + step, :] for s in range(STORED)]
        for k in range(SLOTS):
            total = jnp.where(hits[k][0], blocks[0], 0.0)
            for s in range(1, STORED):
                total = total + jnp.where(hits[k][s], blocks[s], 0.0)
            high = total.astype(jnp.bfloat16)
            low = (total - high.astype(jnp.float32)).astype(jnp.bfloat16)
            write(r, step, k, high, low)


def kernel(
    vals, bcols, rcols, out,
    abuf, bbuf, ad, bhi, blo, cacc, crecv, ostg,
    stage_sem, za_send, za_recv, y_send, y_recv, x_send, x_recv, s_send, s_recv, c_send, c_recv, o_sem,
):
    row, col = lax.axis_index("row"), lax.axis_index("col")
    x, yh, c = lax.div(row, 4), lax.rem(lax.div(row, 2), 2), lax.rem(row, 2)
    z, yl = lax.div(col, 2), lax.rem(col, 2)

    def at_row(x_, yh_, c_):
        return (x_ * 2 + yh_) * 2 + c_

    z_up, z_down = lax.rem(z + 1, NZ), lax.rem(z + NZ - 1, NZ)
    x_up, x_down = lax.rem(x + 1, NX), lax.rem(x + NX - 1, NX)
    sibling = (at_row(x, yh, 1 - c), col)
    partner = (row, z * 2 + 1 - yl)
    z_side = ((row, z_up * 2 + yl), (row, z_down * 2 + yl))
    alone = jnp.logical_and(yh == c, c == yl)

    for p in range(ROWS):
        pltpu.make_async_copy(
            vals.at[p], abuf.at[z, p, pl.ds(0, BODY)], stage_sem.at[p]
        ).start()

    barrier = pltpu.get_barrier_semaphore()

    def greet(device):
        pl.semaphore_signal(barrier, inc=1, device_id=device, device_id_type=MESH)

    greet(z_side[0])
    greet(z_side[1])
    greet((at_row(x_up, yh, c), col))
    greet((at_row(x_down, yh, c), col))
    greet(sibling)
    greet(partner)
    for k in range(2):
        @pl.when(jnp.logical_not(jnp.logical_and(alone, yh == k)))
        def _():
            greet((at_row(x, k, yh), z * 2 + c))
            greet((at_row(x, c, yl), z * 2 + k))

    for p in range(ROWS):
        head = [
            jnp.full((1, ORDER), bcols[p, 0, s].astype(jnp.float32)) for s in range(STORED)
        ]
        head = head + [jnp.zeros((8 - STORED, ORDER), jnp.float32)]
        abuf[z, p, BODY:PIECE, :] = jnp.concatenate(head, axis=0)
    for p in range(ROWS):
        pltpu.make_async_copy(
            vals.at[p], abuf.at[z, p, pl.ds(0, BODY)], stage_sem.at[p]
        ).wait()
    pl.semaphore_wait(barrier, jnp.where(alone, 8, 10))

    def z_copy(way, n, back):
        p, m = lax.div(n, 7), lax.rem(n, 7)
        far = lax.div(m, 2) + back
        source = lax.rem(z + (NZ - far if way == 0 else far), NZ)
        for parity in range(2):
            first = parity if way == 0 else 1 - parity
            rows = pl.ds(0, CUT) if first == 0 else pl.ds(CUT, PIECE - CUT)
            ref = abuf.at[source, p, rows]
            yield lax.rem(m, 2) == parity, pltpu.make_async_remote_copy(
                src_ref=ref,
                dst_ref=ref,
                send_sem=za_send.at[way, n],
                recv_sem=za_recv.at[way, n],
                device_id=z_side[way],
                device_id_type=MESH,
            )

    def z_start(way, n):
        for when, copy in z_copy(way, n, 0):
            pl.when(when)(copy.start)

    def z_arrive(way, n):
        for when, copy in z_copy(way, n, 1):
            pl.when(when)(copy.wait_recv)

    def z_sent(way, n):
        for when, copy in z_copy(way, n, 0):
            pl.when(when)(copy.wait_send)

    def turn(i):
        return 1 - 2 * lax.rem(c + lax.div(i, ROWS), 2)

    def along_x(steps):
        return lax.rem(x + steps + 2 * NX, NX)

    def x_copy(role, i):
        t = turn(i)
        source = along_x(-t) if role == 2 else x
        target = along_x(-t) if role == 1 else along_x(t)
        ref = bbuf.at[i, source * 2 + c]
        return pltpu.make_async_remote_copy(
            src_ref=ref,
            dst_ref=ref,
            send_sem=x_send.at[role, i],
            recv_sem=x_recv.at[role, i],
            device_id=(at_row(target, yh, c), col),
            device_id_type=MESH,
        )

    def x_source(role, i):
        t = turn(i)
        return (along_x(-t), along_x(t), along_x(2), x)[role]

    def x_arrive(role, i):
        ref = bbuf.at[i, x_source(role, i) * 2 + c]
        pltpu.make_async_remote_copy(
            src_ref=ref,
            dst_ref=ref,
            send_sem=x_send.at[role, i],
            recv_sem=x_recv.at[role, i],
            device_id=(at_row(x_up, yh, c), col),
            device_id_type=MESH,
        ).wait_recv()

    def s_copy(role, i):
        ref = bbuf.at[i, x_source(role, i) * 2 + c]
        return pltpu.make_async_remote_copy(
            src_ref=ref,
            dst_ref=ref,
            send_sem=s_send.at[role, i],
            recv_sem=s_recv.at[role, i],
            device_id=sibling,
            device_id_type=MESH,
        )

    def s_arrive(role, i):
        source = (x_source(1, i), x_source(0, i), along_x(2), x)[role]
        ref = bbuf.at[i, source * 2 + 1 - c]
        pltpu.make_async_remote_copy(
            src_ref=ref,
            dst_ref=ref,
            send_sem=s_send.at[role, i],
            recv_sem=s_recv.at[role, i],
            device_id=sibling,
            device_id_type=MESH,
        ).wait_recv()

    def y_copy(k, p):
        i = jnp.where(c == yl, ROWS, 0) + p
        return pltpu.make_async_remote_copy(
            src_ref=abuf.at[z, p],
            dst_ref=bbuf.at[i, x * 2 + yh],
            send_sem=y_send.at[k, p],
            recv_sem=y_recv.at[i],
            device_id=(at_row(x, k, yh), z * 2 + c),
            device_id_type=MESH,
        )

    def y_local(p):
        return pltpu.make_async_copy(
            abuf.at[z, p], bbuf.at[ROWS + p, x * 2 + yh], y_recv.at[ROWS + p]
        )

    def y_start():
        @pl.loop(0, ROWS)
        def _(p):
            for k in range(2):
                here = jnp.logical_and(alone, yh == k)
                pl.when(here)(lambda: y_local(p).start())
                pl.when(jnp.logical_not(here))(lambda: y_copy(k, p).start())

    def y_arrive(i):
        ref = bbuf.at[i, x * 2 + c]
        own = jnp.logical_and(alone, i >= ROWS)

        @pl.when(own)
        def _():
            y_local(lax.rem(i, ROWS)).wait()

        @pl.when(jnp.logical_not(own))
        def _():
            pltpu.make_async_remote_copy(
                src_ref=ref,
                dst_ref=ref,
                send_sem=y_send.at[0, 0],
                recv_sem=y_recv.at[i],
                device_id=sibling,
                device_id_type=MESH,
            ).wait_recv()

    def c_copy(p):
        return pltpu.make_async_remote_copy(
            src_ref=cacc.at[p],
            dst_ref=crecv.at[p],
            send_sem=c_send.at[p],
            recv_sem=c_recv.at[p],
            device_id=partner,
            device_id_type=MESH,
        )

    def spread_left(source, p):
        lanes = pl.multiple_of(source * 2 * ORDER, 2 * ORDER)

        def write(r, step, k, high, low):
            at = pl.ds(lanes + (k % 2) * ORDER, ORDER)
            ad[p * 2 + k // 2, r : r + step, at] = high
            ad[p * 2 + k // 2, ORDER + r : ORDER + r + step, at] = low

        spread(abuf.at[source, p], write)

    def spread_right(i, slot):
        base = pl.multiple_of(slot * 2 * ORDER + lax.rem(i, 2) * ORDER, ORDER)

        def write(r, step, k, high, low):
            rows = pl.ds(base + r, step)
            cols = pl.ds(k * ORDER, ORDER)
            bhi[lax.div(i, 2), rows, cols] = high
            blo[lax.div(i, 2), rows, cols] = low

        spread(bbuf.at[i, slot], write)

    def product(p, phase, half):
        left = ad.at[p * 2 + half]
        both = jnp.dot(left[...], bhi[phase * 2 + half], preferred_element_type=jnp.float32)
        rest = jnp.dot(left[0:ORDER, :], blo[phase * 2 + half], preferred_element_type=jnp.float32)
        total = both[0:ORDER] + (both[ORDER:] + rest)
        at = phase * ROWS + p
        cacc[at] = jnp.where(half == 0, 0.0, cacc[at]) + total

    for n in range(2):
        for way in range(2):
            z_start(way, jnp.int32(n))

    @pl.loop(0, STEPS)
    def _(n):
        p, m = lax.div(n, 7), lax.rem(n, 7)
        third = lax.rem(n, 3)

        @pl.when(n == jnp.where(c == yl, 4, 0))
        def _():
            y_start()

        @pl.when(n < RING)
        def _():
            for way in range(2):
                z_arrive(way, n)

                @pl.when(n + 2 < RING)
                def _():
                    z_start(way, n + 2)

        y_now = jnp.logical_or(n < ROWS, jnp.logical_and(n >= 2 * ROWS, n < 3 * ROWS))

        @pl.when(y_now)
        def _():
            i = jnp.where(n < ROWS, n, n - ROWS)
            y_arrive(i)
            x_copy(0, i).start()
            x_copy(1, i).start()
            s_copy(3, i).start()

        @pl.when(jnp.logical_and(third == 2, n <= 23))
        def _():
            i = lax.div(n, 3)
            x_arrive(0, i)
            x_copy(2, i).start()
            x_arrive(1, i)
            s_copy(0, i).start()
            s_copy(1, i).start()

        @pl.when(jnp.logical_and(third == 1, jnp.logical_and(n >= 4, n <= 25)))
        def _():
            i = lax.div(n, 3) - 1
            x_arrive(2, i)
            s_copy(2, i).start()

        near = jnp.logical_and(third == 0, jnp.logical_and(n >= 3, n <= 24))
        rest = jnp.logical_and(third == 2, jnp.logical_and(n >= 5, n <= 26))
        i_right = jnp.clip(lax.div(n, 3) - 1, 0, 2 * ROWS - 1)

        @pl.when(near)
        def _():
            s_arrive(0, i_right)
            s_arrive(1, i_right)

        @pl.when(rest)
        def _():
            s_arrive(2, i_right)
            s_arrive(3, i_right)

        @pl.when(jnp.logical_or(near, rest))
        def _():
            @pl.loop(0, 4)
            def _(k):
                away = lax.rem(k, 2) * 2 + jnp.where(near, 1, 0)
                spread_right(i_right, along_x(away) * 2 + lax.div(k, 2))

        @pl.when(n < RING)
        def _():
            far = jnp.where(m == 0, 0, lax.div(m + 2, 2))
            count = jnp.where(
                jnp.logical_or(m == 0, m == 6), 1, jnp.where(lax.rem(m, 2) == 1, 2, 0)
            )

            @pl.loop(0, count)
            def _(k):
                source = lax.rem(z + jnp.where(k == 0, far, NZ - far), NZ)
                spread_left(source, p)

        code = jnp.int32(0)
        for at, left_row, phase, half in PRODUCTS:
            code = code + jnp.where(n == at, 1 + left_row * 4 + phase * 2 + half, 0)

        @pl.when(code > 0)
        def _():
            unit = jnp.maximum(code - 1, 0)
            left_row, phase, half = lax.div(unit, 4), lax.rem(lax.div(unit, 2), 2), lax.rem(unit, 2)
            product(left_row, phase, half)

            @pl.when(jnp.logical_and(phase == 0, half == 1))
            def _():
                c_copy(left_row).start()

    @pl.loop(0, ROWS)
    def _(p):
        c_copy(p).wait_recv()
        for u in range(SLOTS):
            want = rcols[p, 0, u]
            for r in range(0, ORDER, 32):
                rows = slice(r, r + 32)
                block = jnp.zeros((32, ORDER), jnp.float32)
                for k in range(SLOTS):
                    cols = slice(k * ORDER, (k + 1) * ORDER)
                    both = cacc[ROWS + p, rows, cols] + crecv[p, rows, cols]
                    block = jnp.where(want == k, both, block)
                ostg[p, u, rows, :] = block
        pltpu.make_async_copy(ostg.at[p], out.at[p, 0], o_sem.at[p]).start()

    @pl.loop(0, RING)
    def _(n):
        for way in range(2):
            z_sent(way, n)

    @pl.loop(0, ROWS)
    def _(p):
        for k in range(2):
            pl.when(jnp.logical_not(jnp.logical_and(alone, yh == k)))(
                lambda: y_copy(k, p).wait_send()
            )
        c_copy(p).wait_send()

    @pl.loop(0, 2 * ROWS)
    def _(i):
        for role in range(3):
            x_copy(role, i).wait_send()
        for role in range(4):
            s_copy(role, i).wait_send()

    @pl.loop(0, ROWS)
    def _(p):
        pltpu.make_async_copy(ostg.at[p], out.at[p, 0], o_sem.at[p]).wait()


def on_device(block_values, block_cols, result_cols):
    vals = block_values.reshape(ROWS, BODY, ORDER)
    dma = pltpu.SemaphoreType.DMA
    return pl.pallas_call(
        kernel,
        out_shape=jax.ShapeDtypeStruct((ROWS, 1, SLOTS, ORDER, ORDER), jnp.float32),
        in_specs=[
            pl.BlockSpec(memory_space=pl.ANY),
            pl.BlockSpec(memory_space=pltpu.SMEM),
            pl.BlockSpec(memory_space=pltpu.SMEM),
        ],
        out_specs=pl.BlockSpec(memory_space=pl.ANY),
        scratch_shapes=[
            pltpu.VMEM((NZ, ROWS, PIECE, ORDER), jnp.float32),
            pltpu.VMEM((2 * ROWS, 2 * NX, PIECE, ORDER), jnp.float32),
            pltpu.VMEM((2 * ROWS, 2 * ORDER, NZ * 2 * ORDER), jnp.bfloat16),
            pltpu.VMEM((4, NZ * 2 * ORDER, SLOTS * ORDER), jnp.bfloat16),
            pltpu.VMEM((4, NZ * 2 * ORDER, SLOTS * ORDER), jnp.bfloat16),
            pltpu.VMEM((2 * ROWS, ORDER, SLOTS * ORDER), jnp.float32),
            pltpu.VMEM((ROWS, ORDER, SLOTS * ORDER), jnp.float32),
            pltpu.VMEM((ROWS, SLOTS, ORDER, ORDER), jnp.float32),
            dma((ROWS,)),
            dma((2, RING)),
            dma((2, RING)),
            dma((2, ROWS)),
            dma((2 * ROWS,)),
            dma((3, 2 * ROWS)),
            dma((3, 2 * ROWS)),
            dma((4, 2 * ROWS)),
            dma((4, 2 * ROWS)),
            dma((ROWS,)),
            dma((ROWS,)),
            dma((ROWS,)),
        ],
        compiler_params=pltpu.CompilerParams(
            collective_id=0, has_side_effects=True, vmem_limit_bytes=60 * 2**20
        ),
    )(vals, block_cols, result_cols)


def solution(mesh):
    return jax.shard_map(
        on_device,
        mesh=mesh,
        in_specs=(P("row", "col", None, None, None), P("row", "col", None), P("row", "col", None)),
        out_specs=P("row", "col", None, None, None),
        check_vma=False,
    )
```

time: 700 us -> 107 us (0.15)
  matrix products: 191 us -> 0 us
  starting transfers between devices: 173 us -> 0 us
  waiting for transfers between devices: 171 us -> 0 us
  local copies, waits for them, and re-layouts: 155 us -> 3.64 us
  Pallas kernels: 0 us -> 103 us
    dot_general x32 -> x0, matrix products: 191 us -> none  [the longest x16 107 us: multiply_pieces(): jnp.einsum('imxy,imnyz->imnxz', left_flat, chosen_blocks, precision=lax.P...]
    ppermute x76 -> x0, starting transfers between devices: 173 us -> none  [passed_along(): return lax.ppermute(value, axis, pairs)]
    ppermute x76 -> x0, waiting for transfers between devices: 171 us -> none  [passed_along(): return lax.ppermute(value, axis, pairs)]
    pallas_call x0 -> x1, Pallas kernels: none -> 103 us  [on_device(): pl.pallas_call(kernel, out_shape=jax.ShapeDtypeStruct((ROWS, 1, SLOTS, OR...]
    while x60 -> x0, local copies, waits for them, and re-layouts: 62.3 us -> none
    dot_general x16 -> x0, local copies, waits for them, and re-layouts: 50.4 us -> none  [multiply_pieces(): jnp.einsum('imxy,imnyz->imnxz', left_flat, chosen_blocks, precision=lax.P...]
    gather x48 -> x0, local copies, waits for them, and re-layouts: 38.4 us -> none  [the longest x16 29.3 us: multiply_pieces(): chosen_blocks = right_flat[inner_rows]]
  transfers between devices with their start and end apart: 76 -> 0, of which waited for: 16 -> 0; matrix products, arithmetic and copies ran while one was open for 43% -> 0% of each run, Pallas kernels for 0% -> 0%
where the time goes in v1:
time: 107 us
  Pallas kernels  103 us (96%)
  local copies, waits for them, and re-layouts  3.64 us (3%)
    pallas_call x1, Pallas kernels, on_device(): pl.pallas_call(kernel, out_shape=jax.ShapeDtypeStruct((ROWS, 1, SLOTS, OR...  103 us
    unnamed x4, local copies, waits for them, and re-layouts  3.64 us

profile of v1, /device:TPU:1, one launch (start us, length us, event | category | flops | bytes accessed | tf_op | source)
XLA Modules:
  0.0 107.1 jit_solution(5426401580021924171)
XLA Ops:
  0.0 0.0 copy-start
  0.0 0.7 copy-done
  0.7 0.7 copy.4.bcols
  1.3 103.4 %shard_map.37 = f32[4,1,4,128,128]{4,3,2,1,0:T(8,128)} custom-call(f32[4,384,128]{2,1,0:T(8,128)} %bitcast.1, s32[4,1,3]{2,1,0:T(1,128)} %copy.4.bcols, s32[4,1,4]{2,1,0:T(1,128)} %rcols.1), custom_call_target="tpu_custom_call" | custom-call | tf_op jit(solution)/shard_map/pallas_call | solution.py:417
  104.8 2.3 %copy.6 = f32[4,1,4,128,128]{4,3,2,1,0:T(8,128)} copy(f32[4,1,4,128,128]{4,3,2,1,0:T(8,128)} %shard_map.37) | data formatting | bytes 2097152
Async XLA Ops:
  0.0 0.7 copy-start

commit v2 on v1

--- a/solution.py
+++ b/solution.py
@@ -14,18 +14,20 @@
 BODY = STORED * ORDER
 PIECE = BODY + 8
 CUT = 192
-RING = 7 * ROWS
+CHAIN = 14
+RING = 2 * CHAIN
+PHASE = 3 * ROWS
 STEPS = 35
 
 PRODUCTS = (
-    (9, 0, 0, 0),
+    (10, 0, 0, 0),
     (15, 0, 0, 1),
     (16, 1, 0, 0),
     (17, 1, 0, 1),
-    (21, 2, 0, 0),
-    (22, 2, 0, 1),
-    (23, 0, 1, 0),
-    (24, 1, 1, 0),
+    (19, 0, 1, 0),
+    (20, 1, 1, 0),
+    (23, 2, 0, 0),
+    (24, 2, 0, 1),
     (25, 2, 1, 0),
     (28, 3, 0, 0),
     (29, 3, 0, 1),
@@ -98,7 +100,7 @@
 
     for p in range(ROWS):
         head = [
-            jnp.full((1, ORDER), bcols[p, 0, s].astype(jnp.float32)) for s in range(STORED)
+            jnp.full((1, ORDER), bcols[s, 0, p].astype(jnp.float32)) for s in range(STORED)
         ]
         head = head + [jnp.zeros((8 - STORED, ORDER), jnp.float32)]
         abuf[z, p, BODY:PIECE, :] = jnp.concatenate(head, axis=0)
@@ -108,8 +110,8 @@
         ).wait()
     pl.semaphore_wait(barrier, jnp.where(alone, 8, 10))
 
-    def z_copy(way, n, back):
-        p, m = lax.div(n, 7), lax.rem(n, 7)
+    def z_copy(way, chain, at, back):
+        p, m = lax.div(at, 7) * 2 + chain, lax.rem(at, 7)
         far = lax.div(m, 2) + back
         source = lax.rem(z + (NZ - far if way == 0 else far), NZ)
         for parity in range(2):
@@ -119,81 +121,53 @@
             yield lax.rem(m, 2) == parity, pltpu.make_async_remote_copy(
                 src_ref=ref,
                 dst_ref=ref,
-                send_sem=za_send.at[way, n],
-                recv_sem=za_recv.at[way, n],
+                send_sem=za_send.at[way, chain * CHAIN + at],
+                recv_sem=za_recv.at[way, chain * CHAIN + at],
                 device_id=z_side[way],
                 device_id_type=MESH,
             )
 
-    def z_start(way, n):
-        for when, copy in z_copy(way, n, 0):
+    def z_start(way, chain, at):
+        for when, copy in z_copy(way, chain, at, 0):
             pl.when(when)(copy.start)
 
-    def z_arrive(way, n):
-        for when, copy in z_copy(way, n, 1):
+    def z_arrive(way, chain, at):
+        for when, copy in z_copy(way, chain, at, 1):
             pl.when(when)(copy.wait_recv)
 
-    def z_sent(way, n):
-        for when, copy in z_copy(way, n, 0):
+    def z_sent(way, chain, at):
+        for when, copy in z_copy(way, chain, at, 0):
             pl.when(when)(copy.wait_send)
 
-    def turn(i):
-        return 1 - 2 * lax.rem(c + lax.div(i, ROWS), 2)
+    turn = 1 - 2 * c
 
     def along_x(steps):
-        return lax.rem(x + steps + 2 * NX, NX)
-
-    def x_copy(role, i):
-        t = turn(i)
-        source = along_x(-t) if role == 2 else x
-        target = along_x(-t) if role == 1 else along_x(t)
-        ref = bbuf.at[i, source * 2 + c]
+        return lax.rem(x + steps + 4 * NX, NX)
+
+    def x_copy(k, back):
+        i = lax.div(k, PHASE) * ROWS + lax.rem(k, ROWS)
+        far = lax.div(lax.rem(k, PHASE), ROWS) + back
+        ref = bbuf.at[i, along_x(-turn * far) * 2 + c]
         return pltpu.make_async_remote_copy(
             src_ref=ref,
             dst_ref=ref,
-            send_sem=x_send.at[role, i],
-            recv_sem=x_recv.at[role, i],
-            device_id=(at_row(target, yh, c), col),
+            send_sem=x_send.at[k],
+            recv_sem=x_recv.at[k],
+            device_id=(at_row(along_x(turn), yh, c), col),
             device_id_type=MESH,
         )
 
-    def x_source(role, i):
-        t = turn(i)
-        return (along_x(-t), along_x(t), along_x(2), x)[role]
-
-    def x_arrive(role, i):
-        ref = bbuf.at[i, x_source(role, i) * 2 + c]
-        pltpu.make_async_remote_copy(
-            src_ref=ref,
-            dst_ref=ref,
-            send_sem=x_send.at[role, i],
-            recv_sem=x_recv.at[role, i],
-            device_id=(at_row(x_up, yh, c), col),
-            device_id_type=MESH,
-        ).wait_recv()
-
-    def s_copy(role, i):
-        ref = bbuf.at[i, x_source(role, i) * 2 + c]
+    def s_copy(far, i, back):
+        slot = along_x(turn * far) * 2 + 1 - c if back else along_x(-turn * far) * 2 + c
+        ref = bbuf.at[i, slot]
         return pltpu.make_async_remote_copy(
             src_ref=ref,
             dst_ref=ref,
-            send_sem=s_send.at[role, i],
-            recv_sem=s_recv.at[role, i],
+            send_sem=s_send.at[far, i],
+            recv_sem=s_recv.at[far, i],
             device_id=sibling,
             device_id_type=MESH,
         )
-
-    def s_arrive(role, i):
-        source = (x_source(1, i), x_source(0, i), along_x(2), x)[role]
-        ref = bbuf.at[i, source * 2 + 1 - c]
-        pltpu.make_async_remote_copy(
-            src_ref=ref,
-            dst_ref=ref,
-            send_sem=s_send.at[role, i],
-            recv_sem=s_recv.at[role, i],
-            device_id=sibling,
-            device_id_type=MESH,
-        ).wait_recv()
 
     def y_copy(k, p):
         i = jnp.where(c == yl, ROWS, 0) + p
@@ -249,23 +223,32 @@
         )
 
     def spread_left(source, p):
-        lanes = pl.multiple_of(source * 2 * ORDER, 2 * ORDER)
+        mine = lax.rem(source, 2) == c
+        far = along_x(jnp.where(mine, turn, -turn) * (x - lax.div(source, 2)) - x)
+        lanes = pl.multiple_of(
+            (lax.rem(far, 2) * 2 + jnp.where(mine, 0, 1)) * SLOTS * ORDER, SLOTS * ORDER
+        )
+        unit = p * 2 + lax.div(far, 2)
 
         def write(r, step, k, high, low):
-            at = pl.ds(lanes + (k % 2) * ORDER, ORDER)
-            ad[p * 2 + k // 2, r : r + step, at] = high
-            ad[p * 2 + k // 2, ORDER + r : ORDER + r + step, at] = low
+            at = pl.ds(lanes + k * ORDER, ORDER)
+            ad[unit, r : r + step, at] = high
+            ad[unit, ORDER + r : ORDER + r + step, at] = low
 
         spread(abuf.at[source, p], write)
 
-    def spread_right(i, slot):
-        base = pl.multiple_of(slot * 2 * ORDER + lax.rem(i, 2) * ORDER, ORDER)
+    def spread_right(i, far, other):
+        slot = along_x((2 * other - 1) * turn * far) * 2 + jnp.where(other == 1, 1 - c, c)
+        base = pl.multiple_of(
+            (lax.rem(far, 2) * 2 + other) * SLOTS * ORDER + lax.rem(i, ROWS) * ORDER, ORDER
+        )
+        unit = lax.div(i, ROWS) * 2 + lax.div(far, 2)
 
         def write(r, step, k, high, low):
             rows = pl.ds(base + r, step)
             cols = pl.ds(k * ORDER, ORDER)
-            bhi[lax.div(i, 2), rows, cols] = high
-            blo[lax.div(i, 2), rows, cols] = low
+            bhi[unit, rows, cols] = high
+            blo[unit, rows, cols] = low
 
         spread(bbuf.at[i, slot], write)
 
@@ -277,14 +260,18 @@
         at = phase * ROWS + p
         cacc[at] = jnp.where(half == 0, 0.0, cacc[at]) + total
 
-    for n in range(2):
+    for at in range(2):
         for way in range(2):
-            z_start(way, jnp.int32(n))
+            z_start(way, 0, jnp.int32(at))
 
     @pl.loop(0, STEPS)
     def _(n):
-        p, m = lax.div(n, 7), lax.rem(n, 7)
-        third = lax.rem(n, 3)
+        even = lax.rem(n, 2) == 0
+        chain = jnp.where(n < 4, 0, jnp.where(n < 24, jnp.where(even, 1, 0), 1))
+        at = jnp.where(
+            n < 4, n, jnp.where(n < 24, lax.div(n + 3, 2) - jnp.where(even, 3, 0), n - CHAIN)
+        )
+        at = jnp.clip(at, 0, CHAIN - 1)
 
         @pl.when(n == jnp.where(c == yl, 4, 0))
         def _():
@@ -293,60 +280,61 @@
         @pl.when(n < RING)
         def _():
             for way in range(2):
-                z_arrive(way, n)
-
-                @pl.when(n + 2 < RING)
+                z_arrive(way, chain, at)
+
+                @pl.when(at + 2 < CHAIN)
                 def _():
-                    z_start(way, n + 2)
-
-        y_now = jnp.logical_or(n < ROWS, jnp.logical_and(n >= 2 * ROWS, n < 3 * ROWS))
-
-        @pl.when(y_now)
-        def _():
-            i = jnp.where(n < ROWS, n, n - ROWS)
+                    z_start(way, chain, at + 2)
+
+                @pl.when(jnp.logical_or(n == 1, n == 2))
+                def _():
+                    z_start(way, 1, n - 1)
+
+        k = n - 3
+
+        @pl.when(jnp.logical_and(k >= 0, k < 2 * PHASE))
+        def _():
+            x_copy(k, 1).wait_recv()
+
+            @pl.when(lax.rem(k, PHASE) < 2 * ROWS)
+            def _():
+                x_copy(k + ROWS, 0).start()
+
+            i = lax.div(k, PHASE) * ROWS + lax.rem(k, ROWS)
+            s_copy(lax.div(lax.rem(k, PHASE), ROWS) + 1, i, 0).start()
+
+        @pl.when(jnp.logical_or(n < ROWS, jnp.logical_and(n >= 11, n < 11 + ROWS)))
+        def _():
+            i = jnp.where(n < ROWS, n, n - 11 + ROWS)
             y_arrive(i)
-            x_copy(0, i).start()
-            x_copy(1, i).start()
-            s_copy(3, i).start()
-
-        @pl.when(jnp.logical_and(third == 2, n <= 23))
-        def _():
-            i = lax.div(n, 3)
-            x_arrive(0, i)
-            x_copy(2, i).start()
-            x_arrive(1, i)
-            s_copy(0, i).start()
-            s_copy(1, i).start()
-
-        @pl.when(jnp.logical_and(third == 1, jnp.logical_and(n >= 4, n <= 25)))
-        def _():
-            i = lax.div(n, 3) - 1
-            x_arrive(2, i)
-            s_copy(2, i).start()
-
-        near = jnp.logical_and(third == 0, jnp.logical_and(n >= 3, n <= 24))
-        rest = jnp.logical_and(third == 2, jnp.logical_and(n >= 5, n <= 26))
-        i_right = jnp.clip(lax.div(n, 3) - 1, 0, 2 * ROWS - 1)
-
-        @pl.when(near)
-        def _():
-            s_arrive(0, i_right)
-            s_arrive(1, i_right)
-
-        @pl.when(rest)
-        def _():
-            s_arrive(2, i_right)
-            s_arrive(3, i_right)
-
-        @pl.when(jnp.logical_or(near, rest))
-        def _():
-            @pl.loop(0, 4)
-            def _(k):
-                away = lax.rem(k, 2) * 2 + jnp.where(near, 1, 0)
-                spread_right(i_right, along_x(away) * 2 + lax.div(k, 2))
+            x_copy(lax.div(i, ROWS) * PHASE + lax.rem(i, ROWS), 0).start()
+            s_copy(0, i, 0).start()
+
+        def both_cores(far, i):
+            s_copy(far, i, 1).wait_recv()
+
+            @pl.loop(0, 2)
+            def _(other):
+                spread_right(i, far, other)
+
+        own = jnp.logical_or(
+            jnp.logical_and(n >= 1, n < 1 + ROWS), jnp.logical_and(n >= 12, n < 12 + ROWS)
+        )
+        came = jnp.logical_and(n >= 4, n < 4 + 2 * PHASE)
+        k_came = jnp.clip(n - 4, 0, 2 * PHASE - 1)
+        i_own = jnp.where(n < 1 + ROWS, jnp.maximum(n - 1, 0), n - 12 + ROWS)
+        i_came = lax.div(k_came, PHASE) * ROWS + lax.rem(k_came, ROWS)
+
+        @pl.loop(jnp.where(own, 0, 1), jnp.where(came, 2, 1))
+        def _(j):
+            both_cores(
+                jnp.where(j == 0, 0, lax.div(lax.rem(k_came, PHASE), ROWS) + 1),
+                jnp.where(j == 0, i_own, i_came),
+            )
 
         @pl.when(n < RING)
         def _():
+            p, m = lax.div(at, 7) * 2 + chain, lax.rem(at, 7)
             far = jnp.where(m == 0, 0, lax.div(m + 2, 2))
             count = jnp.where(
                 jnp.logical_or(m == 0, m == 6), 1, jnp.where(lax.rem(m, 2) == 1, 2, 0)
@@ -386,10 +374,11 @@
                 ostg[p, u, rows, :] = block
         pltpu.make_async_copy(ostg.at[p], out.at[p, 0], o_sem.at[p]).start()
 
-    @pl.loop(0, RING)
+    @pl.loop(0, CHAIN)
     def _(n):
         for way in range(2):
-            z_sent(way, n)
+            for chain in range(2):
+                z_sent(way, chain, n)
 
     @pl.loop(0, ROWS)
     def _(p):
@@ -401,10 +390,10 @@
 
     @pl.loop(0, 2 * ROWS)
     def _(i):
-        for role in range(3):
-            x_copy(role, i).wait_send()
-        for role in range(4):
-            s_copy(role, i).wait_send()
+        for far in range(3):
+            x_copy(lax.div(i, ROWS) * PHASE + far * ROWS + lax.rem(i, ROWS), 0).wait_send()
+        for far in range(4):
+            s_copy(far, i, 0).wait_send()
 
     @pl.loop(0, ROWS)
     def _(p):
@@ -437,8 +426,8 @@
             dma((2, RING)),
             dma((2, ROWS)),
             dma((2 * ROWS,)),
-            dma((3, 2 * ROWS)),
-            dma((3, 2 * ROWS)),
+            dma((2 * PHASE,)),
+            dma((2 * PHASE,)),
             dma((4, 2 * ROWS)),
             dma((4, 2 * ROWS)),
             dma((ROWS,)),
@@ -448,7 +437,7 @@
         compiler_params=pltpu.CompilerParams(
             collective_id=0, has_side_effects=True, vmem_limit_bytes=60 * 2**20
         ),
-    )(vals, block_cols, result_cols)
+    )(vals, jnp.transpose(block_cols, (2, 1, 0)), result_cols)
 
 
 def solution(mesh):

time: 107 us -> 87.2 us (0.81)
  Pallas kernels: 103 us -> 84.8 us
  local copies, waits for them, and re-layouts: 3.64 us -> 2.3 us
    pallas_call x1, Pallas kernels: 103 us -> 84.8 us  [on_device(): pl.pallas_call(kernel, out_shape=jax.ShapeDtypeStruct((ROWS, 1, SLOTS, OR...]
    unnamed x4 -> x1, local copies, waits for them, and re-layouts: 3.64 us -> 2.3 us
where the time goes in v2:
time: 87.2 us; the launch traced here: 87.1 us
  Pallas kernels  84.8 us (97%)
  local copies, waits for them, and re-layouts  2.3 us (3%)
    pallas_call x1, Pallas kernels, on_device(): pl.pallas_call(kernel, out_shape=jax.ShapeDtypeStruct((ROWS, 1, SLOTS, OR...  84.8 us
    unnamed x1, local copies, waits for them, and re-layouts  2.3 us

profile of v2, /device:TPU:1, one launch (start us, length us, event | category | flops | bytes accessed | tf_op | source)
XLA Modules:
  0.0 87.1 jit_solution(16272809377501889726)
XLA Ops:
  0.0 84.8 %shard_map.37 = f32[4,1,4,128,128]{4,3,2,1,0:T(8,128)} custom-call(f32[4,384,128]{2,1,0:T(8,128)} %bitcast.2, s32[3,1,4]{2,1,0:T(1,128)} %bitcast.3, s32[4,1,4]{2,1,0:T(1,128)} %rcols.1), custom_call_target="tpu_custom_call" | custom-call | tf_op jit(solution)/shard_map/pallas_call | solution.py:406
  84.8 2.3 %copy.5 = f32[4,1,4,128,128]{4,3,2,1,0:T(8,128)} copy(f32[4,1,4,128,128]{4,3,2,1,0:T(8,128)} %shard_map.37) | data formatting | bytes 2097152

commit v3 on v2

v3 whole, which is shorter than its diff:
```python
import functools

import jax
import jax.numpy as jnp
from jax import lax
from jax.experimental import pallas as pl
from jax.experimental.pallas import tpu as pltpu
from jax.sharding import PartitionSpec as P

MESH = pl.DeviceIdType.MESH
NX, NZ = 4, 8
ORDER = 128
STORED, SLOTS, ROWS = 3, 4, 4
BODY = STORED * ORDER
PIECE = BODY + 8
UNITS = 2 * ROWS
HALF = ORDER // 2
PHASE = 3 * ROWS

ALONG_Z = (
    (
        (0, 0), (5, 0), (1, 0), (0, 1), (2, 0), (1, 1), (0, 2),
        (3, 0), (1, 2), (0, 3), (4, 0), (3, 1), (2, 1), (4, 1),
        (3, 2), (2, 2), (4, 2), (3, 3), (7, 0), (4, 3), (6, 0),
        (7, 1), (5, 1), (6, 1), (7, 2), (5, 2), (6, 2), (7, 3),
    ),
    (
        (1, 0), (0, 0), (2, 0), (1, 1), (0, 1), (3, 0), (1, 2),
        (2, 1), (0, 2), (1, 3), (4, 0), (3, 1), (2, 2), (5, 0),
        (4, 1), (2, 3), (6, 0), (3, 2), (4, 2), (5, 1), (6, 1),
        (7, 0), (5, 2), (6, 2), (7, 1), (5, 3), (6, 3), (7, 2),
    ),
)
RING = len(ALONG_Z[0])
HEAD_HOPS = (4, 3)


def schedule():
    starts = []
    for seq in ALONG_Z:
        at = {part: q for q, part in enumerate(seq)}
        issue, own = -1, []
        for q, (u, d) in enumerate(seq):
            if d > 0:
                issue = at[(u, d - 1)]
            else:
                own.append((issue, u))
        starts.append(sorted(own, key=lambda e: e[0]))
    done = [max(q for seq in ALONG_Z for q, (v, _) in enumerate(seq) if v == u) for u in range(UNITS)]
    done = [max(done[2 * p : 2 * p + 2]) for p in range(ROWS)]
    ready = {(0, 0): 7, (0, 1): 15, (1, 0): 19, (1, 1): 27}
    wanted = [(phase, p, half) for phase in range(2) for p in range(ROWS) for half in range(2)]
    wanted = [w for w in wanted if w[0] == 1 or w[1] < ROWS - 1]
    rows, n = [], 7
    while wanted:
        can = [w for w in wanted if max(done[w[1]], ready[(w[0], w[2])]) <= n]
        if can and n != RING - 1:
            rows.append((n,) + can[0])
            wanted.remove(can[0])
        n += 1
    units = []
    for u in range(UNITS - 2, UNITS):
        units.append((max(u, 16), u, 0))
        for way, seq in enumerate(ALONG_Z):
            units += [
                (max(q, 16), u, (NZ - d - 1 if way == 0 else d + 1) % NZ)
                for q, (v, d) in enumerate(seq)
                if v == u
            ]
    return starts, rows, sorted(units, key=lambda e: e[0]), n


STARTS, ROW_PRODUCTS, UNIT_PRODUCTS, STEPS = schedule()


def lookup(n, values):
    found = jnp.int32(0)
    for at, value in values:
        found = found + jnp.where(n == at, value, 0)
    return found


def before(n, steps):
    count = jnp.int32(0)
    for at in steps:
        count = count + jnp.where(n > at, 1, 0)
    return count


def spread(block, head, rows, write):
    step = 32
    hits = [
        [jnp.broadcast_to(head(s), (step, ORDER)) == float(k) for s in range(STORED)]
        for k in range(SLOTS)
    ]
    for r in range(0, rows, step):
        blocks = [block(s, pl.ds(r, step)) for s in range(STORED)]
        for k in range(SLOTS):
            total = jnp.where(hits[k][0], blocks[0], 0.0)
            for s in range(1, STORED):
                total = total + jnp.where(hits[k][s], blocks[s], 0.0)
            high = total.astype(jnp.bfloat16)
            low = (total - high.astype(jnp.float32)).astype(jnp.bfloat16)
            write(r, step, k, high, low)


def kernel(
    vals, bcols, rcols, out,
    abuf, hdr, stage, bbuf, ad, bhi, blo, cacc, crecv,
    stage_sem, unit_sem, h_send, h_recv, za_send, za_recv, y_send, y_recv, x_send, x_recv, s_send, s_recv, c_send, c_recv,
):
    row, col = lax.axis_index("row"), lax.axis_index("col")
    x, yh, c = lax.div(row, 4), lax.rem(lax.div(row, 2), 2), lax.rem(row, 2)
    z, yl = lax.div(col, 2), lax.rem(col, 2)

    def at_row(x_, yh_, c_):
        return (x_ * 2 + yh_) * 2 + c_

    z_up, z_down = lax.rem(z + 1, NZ), lax.rem(z + NZ - 1, NZ)
    x_up, x_down = lax.rem(x + 1, NX), lax.rem(x + NX - 1, NX)
    sibling = (at_row(x, yh, 1 - c), col)
    partner = (row, z * 2 + 1 - yl)
    z_side = ((row, z_up * 2 + yl), (row, z_down * 2 + yl))
    alone = jnp.logical_and(yh == c, c == yl)

    def unit_load(u, s):
        p, part = lax.div(u, 2), lax.rem(u, 2)
        rows = pl.ds(pl.multiple_of(s * ORDER + part * HALF, HALF), HALF)
        return pltpu.make_async_copy(
            vals.at[p, rows], abuf.at[z, u, s], unit_sem.at[u, s]
        )

    def row_load(p):
        return pltpu.make_async_copy(
            vals.at[p], stage.at[p, pl.ds(0, BODY)], stage_sem.at[p]
        )

    @pl.loop(0, UNITS)
    def _(u):
        for s in range(STORED):
            unit_load(u, s).start()

    @pl.loop(0, ROWS)
    def _(p):
        row_load(p).start()

    barrier = pltpu.get_barrier_semaphore()

    def greet(device):
        pl.semaphore_signal(barrier, inc=1, device_id=device, device_id_type=MESH)

    greet(z_side[0])
    greet(z_side[1])
    greet((at_row(x_up, yh, c), col))
    greet((at_row(x_down, yh, c), col))
    greet(sibling)
    greet(partner)
    for k in range(2):
        @pl.when(jnp.logical_not(jnp.logical_and(alone, yh == k)))
        def _():
            greet((at_row(x, k, yh), z * 2 + c))
            greet((at_row(x, c, yl), z * 2 + k))

    for p in range(ROWS):
        for s in range(8):
            name = bcols[s, 0, p].astype(jnp.float32) if s < STORED else jnp.float32(0)
            line = jnp.full((1, ORDER), name)
            if s < 4:
                hdr[z, p * 4 + s : p * 4 + s + 1, :] = line
            stage[p, BODY + s : BODY + s + 1, :] = line

    @pl.loop(0, 2 * ROWS)
    def _(at):
        cacc[at] = jnp.zeros((ORDER, SLOTS * ORDER), jnp.float32)

    @pl.loop(0, UNITS)
    def _(u):
        for s in range(STORED):
            unit_load(u, s).wait()

    @pl.loop(0, ROWS)
    def _(p):
        row_load(p).wait()

    pl.semaphore_wait(barrier, jnp.where(alone, 8, 10))

    def behind(way, far):
        return lax.rem(z + (NZ - far if way == 0 else far), NZ)

    def z_copy(way, u, d, back):
        ref = abuf.at[behind(way, d + back), u]
        return pltpu.make_async_remote_copy(
            src_ref=ref,
            dst_ref=ref,
            send_sem=za_send.at[way, u * 4 + d],
            recv_sem=za_recv.at[way, u * 4 + d],
            device_id=z_side[way],
            device_id_type=MESH,
        )

    def h_copy(way, d, back):
        ref = hdr.at[behind(way, d + back)]
        return pltpu.make_async_remote_copy(
            src_ref=ref,
            dst_ref=ref,
            send_sem=h_send.at[way, d],
            recv_sem=h_recv.at[way, d],
            device_id=z_side[way],
            device_id_type=MESH,
        )

    turn = 1 - 2 * c

    def along_x(steps):
        return lax.rem(x + steps + 4 * NX, NX)

    def x_copy(k, back):
        i = lax.div(k, PHASE) * ROWS + lax.rem(k, ROWS)
        far = lax.div(lax.rem(k, PHASE), ROWS) + back
        ref = bbuf.at[i, along_x(-turn * far) * 2 + c]
        return pltpu.make_async_remote_copy(
            src_ref=ref,
            dst_ref=ref,
            send_sem=x_send.at[k],
            recv_sem=x_recv.at[k],
            device_id=(at_row(along_x(turn), yh, c), col),
            device_id_type=MESH,
        )

    def s_copy(far, i, back):
        slot = along_x(turn * far) * 2 + 1 - c if back else along_x(-turn * far) * 2 + c
        ref = bbuf.at[i, slot]
        return pltpu.make_async_remote_copy(
            src_ref=ref,
            dst_ref=ref,
            send_sem=s_send.at[far, i],
            recv_sem=s_recv.at[far, i],
            device_id=sibling,
            device_id_type=MESH,
        )

    def y_copy(k, p):
        i = jnp.where(c == yl, ROWS, 0) + p
        return pltpu.make_async_remote_copy(
            src_ref=stage.at[p],
            dst_ref=bbuf.at[i, x * 2 + yh],
            send_sem=y_send.at[k, p],
            recv_sem=y_recv.at[i],
            device_id=(at_row(x, k, yh), z * 2 + c),
            device_id_type=MESH,
        )

    def y_local(p):
        return pltpu.make_async_copy(
            stage.at[p], bbuf.at[ROWS + p, x * 2 + yh], y_recv.at[ROWS + p]
        )

    def y_start():
        @pl.loop(0, ROWS)
        def _(p):
            for k in range(2):
                here = jnp.logical_and(alone, yh == k)
                pl.when(here)(lambda: y_local(p).start())
                pl.when(jnp.logical_not(here))(lambda: y_copy(k, p).start())

    def y_arrive(i):
        ref = bbuf.at[i, x * 2 + c]
        own = jnp.logical_and(alone, i >= ROWS)

        @pl.when(own)
        def _():
            y_local(lax.rem(i, ROWS)).wait()

        @pl.when(jnp.logical_not(own))
        def _():
            pltpu.make_async_remote_copy(
                src_ref=ref,
                dst_ref=ref,
                send_sem=y_send.at[0, 0],
                recv_sem=y_recv.at[i],
                device_id=sibling,
                device_id_type=MESH,
            ).wait_recv()

    def half_row(u):
        return pl.ds(pl.multiple_of(lax.rem(u, 2) * HALF, HALF), HALF)

    def c_copy(u):
        return pltpu.make_async_remote_copy(
            src_ref=cacc.at[lax.div(u, 2), half_row(u)],
            dst_ref=crecv.at[lax.div(u, 2), half_row(u)],
            send_sem=c_send.at[u],
            recv_sem=c_recv.at[u],
            device_id=partner,
            device_id_type=MESH,
        )

    def spread_left(u, source):
        p, part = lax.div(u, 2), lax.rem(u, 2)
        high_at = pl.multiple_of(HALF + part * HALF, HALF)
        low_at = pl.multiple_of(part * 3 * HALF, HALF)

        def write(r, step, k, high, low):
            cols = pl.ds(k * ORDER, ORDER)
            ad[p, source, pl.ds(high_at + r, step), cols] = high
            ad[p, source, pl.ds(low_at + r, step), cols] = low

        spread(
            lambda s, rows: abuf[source, u, s, rows, :],
            lambda s: hdr[source, pl.ds(p * 4 + s, 1), :],
            HALF,
            write,
        )

    def right_slot(far, other):
        return along_x((2 * other - 1) * turn * far) * 2 + jnp.where(other == 1, 1 - c, c)

    def spread_right(i, far, other):
        slot = right_slot(far, other)
        base = pl.multiple_of(lax.rem(i, ROWS) * ORDER, ORDER)
        phase = lax.div(i, ROWS)

        def write(r, step, k, high, low):
            rows = pl.ds(base + r, step)
            cols = pl.ds(k * ORDER, ORDER)
            bhi[phase, slot, rows, cols] = high
            blo[phase, slot, rows, cols] = low

        spread(
            lambda s, rows: bbuf[i, slot, pl.ds(s * ORDER + rows.start, rows.size), :],
            lambda s: bbuf[i, slot, BODY + s : BODY + s + 1, :],
            ORDER,
            write,
        )

    def dot(left, right):
        return jnp.dot(left, right, preferred_element_type=jnp.float32)

    def row_product(phase, p, half):
        @pl.loop(0, 4)
        def _(j):
            slot = right_slot(half * 2 + lax.div(j, 2), lax.rem(j, 2))
            both = dot(ad[p, slot], bhi[phase, slot])
            rest = dot(ad[p, slot, HALF : 3 * HALF, :], blo[phase, slot])
            at = phase * ROWS + p
            cacc[at, 0:HALF, :] += both[0:HALF] + both[HALF : 2 * HALF] + rest[0:HALF]
            cacc[at, HALF:ORDER, :] += (
                both[2 * HALF : 3 * HALF] + both[3 * HALF :] + rest[HALF:]
            )

    def unit_product(u, source):
        p, part = lax.div(u, 2), lax.rem(u, 2)
        whole = pl.ds(pl.multiple_of(part * ORDER, ORDER), ORDER)
        highs = pl.ds(pl.multiple_of(HALF + part * HALF, HALF), HALF)
        both = dot(ad[p, source, whole, :], bhi[0, source])
        rest = dot(ad[p, source, highs, :], blo[0, source])
        cacc[p, half_row(u), :] += both[0:HALF] + both[HALF:] + rest

    for way in range(2):
        h_copy(way, 0, 0).start()
    for way in range(2):
        for at, u in STARTS[way]:
            if at < 0:
                z_copy(way, u, 0, 0).start()

    @pl.loop(0, STEPS)
    def _(n):
        arrived = [
            lookup(n, [(q, u * 4 + d) for q, (u, d) in enumerate(seq)]) for seq in ALONG_Z
        ]

        @pl.when(n == jnp.where(c == yl, 4, 0))
        def _():
            y_start()

        for d in range(4):
            @pl.when(n == 3 * d)
            def _():
                for way in range(2):
                    if d < HEAD_HOPS[way]:
                        h_copy(way, d, 1).wait_recv()
                    if d + 1 < HEAD_HOPS[way]:
                        h_copy(way, d + 1, 0).start()

        @pl.when(n < RING)
        def _():
            for way in range(2):
                u, d = lax.div(arrived[way], 4), lax.rem(arrived[way], 4)
                z_copy(way, u, d, 1).wait_recv()
                last = lookup(
                    u, [(v, sum(part[0] == v for part in ALONG_Z[way]) - 1) for v in range(UNITS)]
                )

                @pl.when(d < last)
                def _():
                    z_copy(way, u, d + 1, 0).start()

                steps = [at for at, _ in STARTS[way]]

                @pl.loop(before(n, steps), before(n + 1, steps))
                def _(j):
                    own = lookup(j, [(e, v) for e, (_, v) in enumerate(STARTS[way])])
                    z_copy(way, own, 0, 0).start()

        k = n - 3

        @pl.when(jnp.logical_and(k >= 0, k < 2 * PHASE))
        def _():
            x_copy(k, 1).wait_recv()

            @pl.when(lax.rem(k, PHASE) < 2 * ROWS)
            def _():
                x_copy(k + ROWS, 0).start()

            i = lax.div(k, PHASE) * ROWS + lax.rem(k, ROWS)
            s_copy(lax.div(lax.rem(k, PHASE), ROWS) + 1, i, 0).start()

        @pl.when(jnp.logical_or(n < ROWS, jnp.logical_and(n >= 11, n < 11 + ROWS)))
        def _():
            i = jnp.where(n < ROWS, n, n - 11 + ROWS)
            y_arrive(i)
            x_copy(lax.div(i, ROWS) * PHASE + lax.rem(i, ROWS), 0).start()
            s_copy(0, i, 0).start()

        def both_cores(far, i):
            s_copy(far, i, 1).wait_recv()

            @pl.loop(0, 2)
            def _(other):
                spread_right(i, far, other)

        own = jnp.logical_or(
            jnp.logical_and(n >= 1, n < 1 + ROWS), jnp.logical_and(n >= 12, n < 12 + ROWS)
        )
        came = jnp.logical_and(n >= 4, n < 4 + 2 * PHASE)
        k_came = jnp.clip(n - 4, 0, 2 * PHASE - 1)
        i_own = jnp.where(n < 1 + ROWS, jnp.maximum(n - 1, 0), n - 12 + ROWS)
        i_came = lax.div(k_came, PHASE) * ROWS + lax.rem(k_came, ROWS)

        @pl.loop(jnp.where(own, 0, 1), jnp.where(came, 2, 1))
        def _(j):
            both_cores(
                jnp.where(j == 0, 0, lax.div(lax.rem(k_came, PHASE), ROWS) + 1),
                jnp.where(j == 0, i_own, i_came),
            )

        @pl.loop(jnp.where(n < RING, 0, 3), jnp.where(n < UNITS, 3, jnp.where(n < RING, 2, 3)))
        def _(j):
            part = jnp.where(j == 0, arrived[0], jnp.where(j == 1, arrived[1], n * 4))
            far = lax.rem(part, 4) + 1
            away = jnp.where(j == 0, NZ - far, jnp.where(j == 1, far, 0))
            spread_left(lax.div(part, 4), lax.rem(z + away, NZ))

        steps = [at for at, _, _ in UNIT_PRODUCTS]

        @pl.loop(before(n, steps), before(n + 1, steps))
        def _(j):
            code = lookup(j, [(e, u * NZ + a) for e, (_, u, a) in enumerate(UNIT_PRODUCTS)])
            unit_product(lax.div(code, NZ), lax.rem(z + lax.rem(code, NZ), NZ))

        for u in range(UNITS - 2, UNITS):
            @pl.when(n == max(at for at, v, _ in UNIT_PRODUCTS if v == u))
            def _():
                c_copy(u).start()

        code = lookup(n, [(at, 1 + phase * 8 + p * 2 + half) for at, phase, p, half in ROW_PRODUCTS])

        @pl.when(code > 0)
        def _():
            unit = jnp.maximum(code - 1, 0)
            phase, p, half = lax.div(unit, 8), lax.rem(lax.div(unit, 2), ROWS), lax.rem(unit, 2)
            row_product(phase, p, half)

            @pl.when(jnp.logical_and(phase == 0, half == 1))
            def _():
                c_copy(p * 2).start()
                c_copy(p * 2 + 1).start()

    for way in range(2):
        for d in range(HEAD_HOPS[way]):
            h_copy(way, d, 0).wait_send()

        @pl.loop(0, RING)
        def _(n):
            part = lookup(n, [(q, u * 4 + d) for q, (u, d) in enumerate(ALONG_Z[way])])
            z_copy(way, lax.div(part, 4), lax.rem(part, 4), 0).wait_send()

    @pl.loop(0, ROWS)
    def _(p):
        for k in range(2):
            pl.when(jnp.logical_not(jnp.logical_and(alone, yh == k)))(
                lambda: y_copy(k, p).wait_send()
            )

    @pl.loop(0, 2 * ROWS)
    def _(i):
        for far in range(3):
            x_copy(lax.div(i, ROWS) * PHASE + far * ROWS + lax.rem(i, ROWS), 0).wait_send()
        for far in range(4):
            s_copy(far, i, 0).wait_send()

    @pl.loop(0, ROWS)
    def _(p):
        c_copy(p * 2).wait_recv()
        c_copy(p * 2 + 1).wait_recv()
        for u in range(SLOTS):
            want = rcols[p, 0, u]
            for r in range(0, ORDER, 32):
                rows = slice(r, r + 32)
                block = jnp.zeros((32, ORDER), jnp.float32)
                for k in range(SLOTS):
                    cols = slice(k * ORDER, (k + 1) * ORDER)
                    both = cacc[ROWS + p, rows, cols] + crecv[p, rows, cols]
                    block = jnp.where(want == k, both, block)
                out[p, 0, u, rows, :] = block

    @pl.loop(0, UNITS)
    def _(u):
        c_copy(u).wait_send()


def on_device(block_values, block_cols, result_cols):
    vals = block_values.reshape(ROWS, BODY, ORDER)
    dma = pltpu.SemaphoreType.DMA
    return pl.pallas_call(
        kernel,
        out_shape=pltpu.VMEM((ROWS, 1, SLOTS, ORDER, ORDER), jnp.float32),
        in_specs=[
            pl.BlockSpec(memory_space=pl.ANY),
            pl.BlockSpec(memory_space=pltpu.SMEM),
            pl.BlockSpec(memory_space=pltpu.SMEM),
        ],
        out_specs=pl.BlockSpec(memory_space=pltpu.VMEM),
        scratch_shapes=[
            pltpu.VMEM((NZ, UNITS, STORED, HALF, ORDER), jnp.float32),
            pltpu.VMEM((NZ, 4 * ROWS, ORDER), jnp.float32),
            pltpu.VMEM((ROWS, PIECE, ORDER), jnp.float32),
            pltpu.VMEM((2 * ROWS, 2 * NX, PIECE, ORDER), jnp.float32),
            pltpu.VMEM((ROWS, NZ, 2 * ORDER, SLOTS * ORDER), jnp.bfloat16),
            pltpu.VMEM((2, NZ, SLOTS * ORDER, SLOTS * ORDER), jnp.bfloat16),
            pltpu.VMEM((2, NZ, SLOTS * ORDER, SLOTS * ORDER), jnp.bfloat16),
            pltpu.VMEM((2 * ROWS, ORDER, SLOTS * ORDER), jnp.float32),
            pltpu.VMEM((ROWS, ORDER, SLOTS * ORDER), jnp.float32),
            dma((ROWS,)),
            dma((UNITS, STORED)),
            dma((2, 4)),
            dma((2, 4)),
            dma((2, 4 * UNITS)),
            dma((2, 4 * UNITS)),
            dma((2, ROWS)),
            dma((2 * ROWS,)),
            dma((2 * PHASE,)),
            dma((2 * PHASE,)),
            dma((4, 2 * ROWS)),
            dma((4, 2 * ROWS)),
            dma((UNITS,)),
            dma((UNITS,)),
        ],
        compiler_params=pltpu.CompilerParams(
            collective_id=0, has_side_effects=True, vmem_limit_bytes=60 * 2**20
        ),
    )(vals, jnp.transpose(block_cols, (2, 1, 0)), result_cols)


def solution(mesh):
    return jax.shard_map(
        on_device,
        mesh=mesh,
        in_specs=(P("row", "col", None, None, None), P("row", "col", None), P("row", "col", None)),
        out_specs=P("row", "col", None, None, None),
        check_vma=False,
    )
```

time: 87.2 us -> 94.2 us (1.080)
  Pallas kernels: 84.8 us -> 93.1 us
  local copies, waits for them, and re-layouts: 2.3 us -> 0.97 us
    pallas_call x1, Pallas kernels: 84.8 us -> 93.1 us  [on_device(): pl.pallas_call(kernel, out_shape=pltpu.VMEM((ROWS, 1, SLOTS, ORDER, ORDER...]
    unnamed x1, local copies, waits for them, and re-layouts: 2.3 us -> 0.97 us
where the time goes in v3:
time: 94.2 us; the launch traced here: 94.1 us
  Pallas kernels  93.1 us (99%)
  local copies, waits for them, and re-layouts  0.97 us (1%)
    pallas_call x1, Pallas kernels, on_device(): pl.pallas_call(kernel, out_shape=pltpu.VMEM((ROWS, 1, SLOTS, ORDER, ORDER...  93.1 us

profile of v3, /device:TPU:1, one launch (start us, length us, event | category | flops | bytes accessed | tf_op | source)
XLA Modules:
  0.0 94.1 jit_solution(6970907698935779154)
XLA Ops:
  0.0 93.1 %shard_map.37 = f32[4,1,4,128,128]{4,3,2,1,0:T(8,128)S(1)} custom-call(f32[4,384,128]{2,1,0:T(8,128)} %bitcast.2, s32[3,1,4]{2,1,0:T(1,128)} %bitcast.3, s32[4,1,4]{2,1,0:T(1,128)} %rcols.1), custom_call_target="tpu_custom_call" | custom-call | tf_op jit(solution)/shard_map/pallas_call | solution.py:525
  93.1 1.0 %copy.5 = f32[4,1,4,128,128]{4,3,2,1,0:T(8,128)} copy(f32[4,1,4,128,128]{4,3,2,1,0:T(8,128)S(1)} %shard_map.37) | data formatting | bytes 2097152

commit v4 on v3

--- a/solution.py
+++ b/solution.py
@@ -16,19 +16,20 @@
 UNITS = 2 * ROWS
 HALF = ORDER // 2
 PHASE = 3 * ROWS
+EARLY = 22
 
 ALONG_Z = (
     (
-        (0, 0), (5, 0), (1, 0), (0, 1), (2, 0), (1, 1), (0, 2),
-        (3, 0), (1, 2), (0, 3), (4, 0), (3, 1), (2, 1), (4, 1),
-        (3, 2), (2, 2), (4, 2), (3, 3), (7, 0), (4, 3), (6, 0),
-        (7, 1), (5, 1), (6, 1), (7, 2), (5, 2), (6, 2), (7, 3),
+        (0, 0), (1, 0), (0, 1), (1, 1), (2, 0), (0, 2), (3, 0),
+        (1, 2), (0, 3), (2, 1), (3, 1), (4, 0), (2, 2), (5, 0),
+        (3, 2), (2, 3), (4, 1), (5, 1), (6, 0), (4, 2), (5, 2),
+        (6, 1), (4, 3), (7, 0), (6, 2), (7, 1), (6, 3), (7, 2),
     ),
     (
-        (1, 0), (0, 0), (2, 0), (1, 1), (0, 1), (3, 0), (1, 2),
-        (2, 1), (0, 2), (1, 3), (4, 0), (3, 1), (2, 2), (5, 0),
-        (4, 1), (2, 3), (6, 0), (3, 2), (4, 2), (5, 1), (6, 1),
-        (7, 0), (5, 2), (6, 2), (7, 1), (5, 3), (6, 3), (7, 2),
+        (1, 0), (0, 0), (1, 1), (0, 1), (3, 0), (1, 2), (2, 0),
+        (0, 2), (1, 3), (3, 1), (2, 1), (5, 0), (3, 2), (4, 0),
+        (2, 2), (3, 3), (5, 1), (4, 1), (7, 0), (5, 2), (6, 0),
+        (4, 2), (5, 3), (7, 1), (6, 1), (7, 2), (6, 2), (7, 3),
     ),
 )
 RING = len(ALONG_Z[0])
@@ -48,16 +49,20 @@
         starts.append(sorted(own, key=lambda e: e[0]))
     done = [max(q for seq in ALONG_Z for q, (v, _) in enumerate(seq) if v == u) for u in range(UNITS)]
     done = [max(done[2 * p : 2 * p + 2]) for p in range(ROWS)]
-    ready = {(0, 0): 7, (0, 1): 15, (1, 0): 19, (1, 1): 27}
-    wanted = [(phase, p, half) for phase in range(2) for p in range(ROWS) for half in range(2)]
-    wanted = [w for w in wanted if w[0] == 1 or w[1] < ROWS - 1]
-    rows, n = [], 7
-    while wanted:
-        can = [w for w in wanted if max(done[w[1]], ready[(w[0], w[2])]) <= n]
-        if can and n != RING - 1:
-            rows.append((n,) + can[0])
-            wanted.remove(can[0])
-        n += 1
+    ready = {(0, 0): 6, (0, 2): 14, (1, 0): 18, (1, 2): 22, (1, 3): 26}
+    wanted = [(0, p, q, 2) for p in range(ROWS - 1) for q in (0, 2)]
+    wanted += [(1, p, 0, 2) for p in range(ROWS - 1)]
+    wanted += [(1, p, q, 1) for q in (2, 3) for p in range(ROWS - 1)]
+    wanted += [(1, ROWS - 1, q, 2) for q in (0, 2)]
+    rows = []
+    for n in range(RING + 1):
+        room = 2 if n < RING else 4 * ROWS * ROWS
+        for w in list(wanted):
+            open_at = max(done[w[1]], *(ready.get((w[0], q), 0) for q in range(w[2], w[2] + w[3])))
+            if open_at <= n and w[3] <= room:
+                rows.append((n,) + w)
+                wanted.remove(w)
+                room -= w[3]
     units = []
     for u in range(UNITS - 2, UNITS):
         units.append((max(u, 16), u, 0))
@@ -67,10 +72,11 @@
                 for q, (v, d) in enumerate(seq)
                 if v == u
             ]
-    return starts, rows, sorted(units, key=lambda e: e[0]), n
-
-
-STARTS, ROW_PRODUCTS, UNIT_PRODUCTS, STEPS = schedule()
+    return starts, rows, sorted(units, key=lambda e: e[0])
+
+
+STARTS, ROW_PRODUCTS, UNIT_PRODUCTS = schedule()
+STEPS = RING + 1
 
 
 def lookup(n, values):
@@ -295,15 +301,26 @@
             device_id_type=MESH,
         )
 
+    def left_slot(source):
+        mine = lax.rem(source, 2) == c
+        far = along_x(jnp.where(mine, turn, -turn) * (x - lax.div(source, 2)) - x)
+        return far * 2 + jnp.where(mine, 0, 1)
+
+    def in_half(slot):
+        return pl.multiple_of(lax.rem(slot, 4) * SLOTS * ORDER, SLOTS * ORDER)
+
     def spread_left(u, source):
         p, part = lax.div(u, 2), lax.rem(u, 2)
         high_at = pl.multiple_of(HALF + part * HALF, HALF)
         low_at = pl.multiple_of(part * 3 * HALF, HALF)
+        slot = left_slot(source)
+        lanes = in_half(slot)
+        unit = p * 2 + lax.div(slot, 4)
 
         def write(r, step, k, high, low):
-            cols = pl.ds(k * ORDER, ORDER)
-            ad[p, source, pl.ds(high_at + r, step), cols] = high
-            ad[p, source, pl.ds(low_at + r, step), cols] = low
+            cols = pl.ds(lanes + k * ORDER, ORDER)
+            ad[unit, pl.ds(high_at + r, step), cols] = high
+            ad[unit, pl.ds(low_at + r, step), cols] = low
 
         spread(
             lambda s, rows: abuf[source, u, s, rows, :],
@@ -317,14 +334,14 @@
 
     def spread_right(i, far, other):
         slot = right_slot(far, other)
-        base = pl.multiple_of(lax.rem(i, ROWS) * ORDER, ORDER)
-        phase = lax.div(i, ROWS)
+        base = pl.multiple_of(in_half(far * 2 + other) + lax.rem(i, ROWS) * ORDER, ORDER)
+        unit = lax.div(i, ROWS) * 2 + lax.div(far, 2)
 
         def write(r, step, k, high, low):
             rows = pl.ds(base + r, step)
             cols = pl.ds(k * ORDER, ORDER)
-            bhi[phase, slot, rows, cols] = high
-            blo[phase, slot, rows, cols] = low
+            bhi[unit, rows, cols] = high
+            blo[unit, rows, cols] = low
 
         spread(
             lambda s, rows: bbuf[i, slot, pl.ds(s * ORDER + rows.start, rows.size), :],
@@ -336,25 +353,41 @@
     def dot(left, right):
         return jnp.dot(left, right, preferred_element_type=jnp.float32)
 
-    def row_product(phase, p, half):
-        @pl.loop(0, 4)
-        def _(j):
-            slot = right_slot(half * 2 + lax.div(j, 2), lax.rem(j, 2))
-            both = dot(ad[p, slot], bhi[phase, slot])
-            rest = dot(ad[p, slot, HALF : 3 * HALF, :], blo[phase, slot])
-            at = phase * ROWS + p
-            cacc[at, 0:HALF, :] += both[0:HALF] + both[HALF : 2 * HALF] + rest[0:HALF]
-            cacc[at, HALF:ORDER, :] += (
-                both[2 * HALF : 3 * HALF] + both[3 * HALF :] + rest[HALF:]
-            )
+    def row_product(phase, p, half, inner):
+        both = dot(ad[p * 2 + half, :, inner], bhi[phase * 2 + half, inner, :])
+        rest = dot(ad[p * 2 + half, HALF : 3 * HALF, inner], blo[phase * 2 + half, inner, :])
+        at = phase * ROWS + p
+        cacc[at, 0:HALF, :] += both[0:HALF] + both[HALF : 2 * HALF] + rest[0:HALF]
+        cacc[at, HALF:ORDER, :] += (
+            both[2 * HALF : 3 * HALF] + both[3 * HALF :] + rest[HALF:]
+        )
 
     def unit_product(u, source):
         p, part = lax.div(u, 2), lax.rem(u, 2)
         whole = pl.ds(pl.multiple_of(part * ORDER, ORDER), ORDER)
         highs = pl.ds(pl.multiple_of(HALF + part * HALF, HALF), HALF)
-        both = dot(ad[p, source, whole, :], bhi[0, source])
-        rest = dot(ad[p, source, highs, :], blo[0, source])
+        slot = left_slot(source)
+        inner = pl.ds(in_half(slot), SLOTS * ORDER)
+        half = lax.div(slot, 4)
+        both = dot(ad[p * 2 + half, whole, inner], bhi[half, inner, :])
+        rest = dot(ad[p * 2 + half, highs, inner], blo[half, inner, :])
         cacc[p, half_row(u), :] += both[0:HALF] + both[HALF:] + rest
+
+    def z_sent(u):
+        for way, seq in enumerate(ALONG_Z):
+            for d in range(sum(part[0] == u for part in seq)):
+                z_copy(way, u, d, 0).wait_send()
+
+    def y_sent(p):
+        for k in range(2):
+            pl.when(jnp.logical_not(jnp.logical_and(alone, yh == k)))(
+                lambda: y_copy(k, p).wait_send()
+            )
+
+    def x_sent(k):
+        x_copy(k, 0).wait_send()
+        i = lax.div(k, PHASE) * ROWS + lax.rem(k, ROWS)
+        s_copy(lax.div(lax.rem(k, PHASE), ROWS) + 1, i, 0).wait_send()
 
     for way in range(2):
         h_copy(way, 0, 0).start()
@@ -374,7 +407,7 @@
             y_start()
 
         for d in range(4):
-            @pl.when(n == 3 * d)
+            @pl.when(n == (0, 2, 5, 8)[d])
             def _():
                 for way in range(2):
                     if d < HEAD_HOPS[way]:
@@ -402,7 +435,7 @@
                     own = lookup(j, [(e, v) for e, (_, v) in enumerate(STARTS[way])])
                     z_copy(way, own, 0, 0).start()
 
-        k = n - 3
+        k = n - 2
 
         @pl.when(jnp.logical_and(k >= 0, k < 2 * PHASE))
         def _():
@@ -415,9 +448,9 @@
             i = lax.div(k, PHASE) * ROWS + lax.rem(k, ROWS)
             s_copy(lax.div(lax.rem(k, PHASE), ROWS) + 1, i, 0).start()
 
-        @pl.when(jnp.logical_or(n < ROWS, jnp.logical_and(n >= 11, n < 11 + ROWS)))
-        def _():
-            i = jnp.where(n < ROWS, n, n - 11 + ROWS)
+        @pl.when(jnp.logical_or(n < ROWS, jnp.logical_and(n >= 10, n < 10 + ROWS)))
+        def _():
+            i = jnp.where(n < ROWS, n, n - 10 + ROWS)
             y_arrive(i)
             x_copy(lax.div(i, ROWS) * PHASE + lax.rem(i, ROWS), 0).start()
             s_copy(0, i, 0).start()
@@ -430,11 +463,11 @@
                 spread_right(i, far, other)
 
         own = jnp.logical_or(
-            jnp.logical_and(n >= 1, n < 1 + ROWS), jnp.logical_and(n >= 12, n < 12 + ROWS)
-        )
-        came = jnp.logical_and(n >= 4, n < 4 + 2 * PHASE)
-        k_came = jnp.clip(n - 4, 0, 2 * PHASE - 1)
-        i_own = jnp.where(n < 1 + ROWS, jnp.maximum(n - 1, 0), n - 12 + ROWS)
+            jnp.logical_and(n >= 1, n < 1 + ROWS), jnp.logical_and(n >= 11, n < 11 + ROWS)
+        )
+        came = jnp.logical_and(n >= 3, n < 3 + 2 * PHASE)
+        k_came = jnp.clip(n - 3, 0, 2 * PHASE - 1)
+        i_own = jnp.where(n < 1 + ROWS, jnp.maximum(n - 1, 0), n - 11 + ROWS)
         i_came = lax.div(k_came, PHASE) * ROWS + lax.rem(k_came, ROWS)
 
         @pl.loop(jnp.where(own, 0, 1), jnp.where(came, 2, 1))
@@ -463,55 +496,81 @@
             def _():
                 c_copy(u).start()
 
-        code = lookup(n, [(at, 1 + phase * 8 + p * 2 + half) for at, phase, p, half in ROW_PRODUCTS])
-
-        @pl.when(code > 0)
-        def _():
-            unit = jnp.maximum(code - 1, 0)
-            phase, p, half = lax.div(unit, 8), lax.rem(lax.div(unit, 2), ROWS), lax.rem(unit, 2)
-            row_product(phase, p, half)
+        for u in range(UNITS - 2):
+            @pl.when(n == 20 + u)
+            def _():
+                z_sent(u)
+
+        @pl.when(jnp.logical_and(n >= 6, n < 6 + EARLY))
+        def _():
+            x_sent(n - 6)
+
+        @pl.when(jnp.logical_and(n >= 18, n < 18 + 2 * ROWS))
+        def _():
+            s_copy(0, n - 18, 0).wait_send()
+
+        @pl.when(jnp.logical_and(n >= 16, n < 16 + ROWS))
+        def _():
+            y_sent(n - 16)
+
+        @pl.when(n == 15)
+        def _():
+            for way in range(2):
+                for d in range(HEAD_HOPS[way]):
+                    h_copy(way, d, 0).wait_send()
+
+        row_steps = [e[0] for e in ROW_PRODUCTS]
+
+        @pl.loop(before(n, row_steps), before(n + 1, row_steps))
+        def _(j):
+            code = lookup(
+                j,
+                [
+                    (e, ((phase * ROWS + p) * 4 + q) * 2 + count - 1)
+                    for e, (_, phase, p, q, count) in enumerate(ROW_PRODUCTS)
+                ],
+            )
+            row, quarter = lax.div(code, 8), lax.rem(lax.div(code, 2), 4)
+            phase, p, half = lax.div(row, ROWS), lax.rem(row, ROWS), lax.div(quarter, 2)
+            depth = 2 * SLOTS * ORDER
+
+            @pl.when(lax.rem(code, 2) == 1)
+            def _():
+                row_product(phase, p, half, pl.ds(0, 2 * depth))
+
+            @pl.when(lax.rem(code, 2) == 0)
+            def _():
+                start = pl.multiple_of(lax.rem(quarter, 2) * depth, depth)
+                row_product(phase, p, half, pl.ds(start, depth))
 
             @pl.when(jnp.logical_and(phase == 0, half == 1))
             def _():
                 c_copy(p * 2).start()
                 c_copy(p * 2 + 1).start()
 
-    for way in range(2):
-        for d in range(HEAD_HOPS[way]):
-            h_copy(way, d, 0).wait_send()
-
-        @pl.loop(0, RING)
-        def _(n):
-            part = lookup(n, [(q, u * 4 + d) for q, (u, d) in enumerate(ALONG_Z[way])])
-            z_copy(way, lax.div(part, 4), lax.rem(part, 4), 0).wait_send()
-
-    @pl.loop(0, ROWS)
-    def _(p):
-        for k in range(2):
-            pl.when(jnp.logical_not(jnp.logical_and(alone, yh == k)))(
-                lambda: y_copy(k, p).wait_send()
-            )
-
-    @pl.loop(0, 2 * ROWS)
-    def _(i):
-        for far in range(3):
-            x_copy(lax.div(i, ROWS) * PHASE + far * ROWS + lax.rem(i, ROWS), 0).wait_send()
-        for far in range(4):
-            s_copy(far, i, 0).wait_send()
+    for u in range(UNITS - 2, UNITS):
+        z_sent(u)
+
+    @pl.loop(EARLY, 2 * PHASE)
+    def _(k):
+        x_sent(k)
 
     @pl.loop(0, ROWS)
     def _(p):
         c_copy(p * 2).wait_recv()
         c_copy(p * 2 + 1).wait_recv()
-        for u in range(SLOTS):
-            want = rcols[p, 0, u]
-            for r in range(0, ORDER, 32):
-                rows = slice(r, r + 32)
-                block = jnp.zeros((32, ORDER), jnp.float32)
-                for k in range(SLOTS):
-                    cols = slice(k * ORDER, (k + 1) * ORDER)
-                    both = cacc[ROWS + p, rows, cols] + crecv[p, rows, cols]
-                    block = jnp.where(want == k, both, block)
+        wants = [rcols[p, 0, u] for u in range(SLOTS)]
+        for r in range(0, ORDER, 32):
+            rows = slice(r, r + 32)
+            both = [
+                cacc[ROWS + p, rows, k * ORDER : (k + 1) * ORDER]
+                + crecv[p, rows, k * ORDER : (k + 1) * ORDER]
+                for k in range(SLOTS)
+            ]
+            for u in range(SLOTS):
+                block = both[0]
+                for k in range(1, SLOTS):
+                    block = jnp.where(wants[u] == k, both[k], block)
                 out[p, 0, u, rows, :] = block
 
     @pl.loop(0, UNITS)
@@ -536,9 +595,9 @@
             pltpu.VMEM((NZ, 4 * ROWS, ORDER), jnp.float32),
             pltpu.VMEM((ROWS, PIECE, ORDER), jnp.float32),
             pltpu.VMEM((2 * ROWS, 2 * NX, PIECE, ORDER), jnp.float32),
-            pltpu.VMEM((ROWS, NZ, 2 * ORDER, SLOTS * ORDER), jnp.bfloat16),
-            pltpu.VMEM((2, NZ, SLOTS * ORDER, SLOTS * ORDER), jnp.bfloat16),
-            pltpu.VMEM((2, NZ, SLOTS * ORDER, SLOTS * ORDER), jnp.bfloat16),
+            pltpu.VMEM((2 * ROWS, 2 * ORDER, 4 * SLOTS * ORDER), jnp.bfloat16),
+            pltpu.VMEM((4, 4 * SLOTS * ORDER, SLOTS * ORDER), jnp.bfloat16),
+            pltpu.VMEM((4, 4 * SLOTS * ORDER, SLOTS * ORDER), jnp.bfloat16),
             pltpu.VMEM((2 * ROWS, ORDER, SLOTS * ORDER), jnp.float32),
             pltpu.VMEM((ROWS, ORDER, SLOTS * ORDER), jnp.float32),
             dma((ROWS,)),

time: 94.2 us -> 86.2 us (0.915)
  Pallas kernels: 93.1 us -> 85.1 us
    pallas_call x1, Pallas kernels: 93.1 us -> 85.1 us  [on_device(): pl.pallas_call(kernel, out_shape=pltpu.VMEM((ROWS, 1, SLOTS, ORDER, ORDER...]
where the time goes in v4:
time: 86.2 us; the launch traced here: 86.1 us
  Pallas kernels  85.1 us (99%)
  local copies, waits for them, and re-layouts  0.97 us (1%)
    pallas_call x1, Pallas kernels, on_device(): pl.pallas_call(kernel, out_shape=pltpu.VMEM((ROWS, 1, SLOTS, ORDER, ORDER...  85.1 us

profile of v4, /device:TPU:1, one launch (start us, length us, event | category | flops | bytes accessed | tf_op | source)
XLA Modules:
  0.0 86.1 jit_solution(17622408171347372628)
XLA Ops:
  0.0 85.1 %shard_map.37 = f32[4,1,4,128,128]{4,3,2,1,0:T(8,128)S(1)} custom-call(f32[4,384,128]{2,1,0:T(8,128)} %bitcast.2, s32[3,1,4]{2,1,0:T(1,128)} %bitcast.3, s32[4,1,4]{2,1,0:T(1,128)} %rcols.1), custom_call_target="tpu_custom_call" | custom-call | tf_op jit(solution)/shard_map/pallas_call | solution.py:584
  85.1 1.0 %copy.5 = f32[4,1,4,128,128]{4,3,2,1,0:T(8,128)} copy(f32[4,1,4,128,128]{4,3,2,1,0:T(8,128)S(1)} %shard_map.37) | data formatting | bytes 2097152

commit v5 on v4

--- a/solution.py
+++ b/solution.py
@@ -94,7 +94,7 @@
 
 
 def spread(block, head, rows, write):
-    step = 32
+    step = 64
     hits = [
         [jnp.broadcast_to(head(s), (step, ORDER)) == float(k) for s in range(STORED)]
         for k in range(SLOTS)
@@ -406,6 +406,13 @@
         def _():
             y_start()
 
+        @pl.when(jnp.logical_or(n < ROWS, jnp.logical_and(n >= 10, n < 10 + ROWS)))
+        def _():
+            i = jnp.where(n < ROWS, n, n - 10 + ROWS)
+            y_arrive(i)
+            x_copy(lax.div(i, ROWS) * PHASE + lax.rem(i, ROWS), 0).start()
+            s_copy(0, i, 0).start()
+
         for d in range(4):
             @pl.when(n == (0, 2, 5, 8)[d])
             def _():
@@ -448,12 +455,24 @@
             i = lax.div(k, PHASE) * ROWS + lax.rem(k, ROWS)
             s_copy(lax.div(lax.rem(k, PHASE), ROWS) + 1, i, 0).start()
 
-        @pl.when(jnp.logical_or(n < ROWS, jnp.logical_and(n >= 10, n < 10 + ROWS)))
-        def _():
-            i = jnp.where(n < ROWS, n, n - 10 + ROWS)
-            y_arrive(i)
-            x_copy(lax.div(i, ROWS) * PHASE + lax.rem(i, ROWS), 0).start()
-            s_copy(0, i, 0).start()
+        @pl.loop(jnp.where(n < RING, 0, 3), jnp.where(n < UNITS, 3, jnp.where(n < RING, 2, 3)))
+        def _(j):
+            part = jnp.where(j == 0, arrived[0], jnp.where(j == 1, arrived[1], n * 4))
+            far = lax.rem(part, 4) + 1
+            away = jnp.where(j == 0, NZ - far, jnp.where(j == 1, far, 0))
+            spread_left(lax.div(part, 4), lax.rem(z + away, NZ))
+
+        steps = [at for at, _, _ in UNIT_PRODUCTS]
+
+        @pl.loop(before(n, steps), before(n + 1, steps))
+        def _(j):
+            code = lookup(j, [(e, u * NZ + a) for e, (_, u, a) in enumerate(UNIT_PRODUCTS)])
+            unit_product(lax.div(code, NZ), lax.rem(z + lax.rem(code, NZ), NZ))
+
+        for u in range(UNITS - 2, UNITS):
+            @pl.when(n == max(at for at, v, _ in UNIT_PRODUCTS if v == u))
+            def _():
+                c_copy(u).start()
 
         def both_cores(far, i):
             s_copy(far, i, 1).wait_recv()
@@ -476,25 +495,6 @@
                 jnp.where(j == 0, 0, lax.div(lax.rem(k_came, PHASE), ROWS) + 1),
                 jnp.where(j == 0, i_own, i_came),
             )
-
-        @pl.loop(jnp.where(n < RING, 0, 3), jnp.where(n < UNITS, 3, jnp.where(n < RING, 2, 3)))
-        def _(j):
-            part = jnp.where(j == 0, arrived[0], jnp.where(j == 1, arrived[1], n * 4))
-            far = lax.rem(part, 4) + 1
-            away = jnp.where(j == 0, NZ - far, jnp.where(j == 1, far, 0))
-            spread_left(lax.div(part, 4), lax.rem(z + away, NZ))
-
-        steps = [at for at, _, _ in UNIT_PRODUCTS]
-
-        @pl.loop(before(n, steps), before(n + 1, steps))
-        def _(j):
-            code = lookup(j, [(e, u * NZ + a) for e, (_, u, a) in enumerate(UNIT_PRODUCTS)])
-            unit_product(lax.div(code, NZ), lax.rem(z + lax.rem(code, NZ), NZ))
-
-        for u in range(UNITS - 2, UNITS):
-            @pl.when(n == max(at for at, v, _ in UNIT_PRODUCTS if v == u))
-            def _():
-                c_copy(u).start()
 
         for u in range(UNITS - 2):
             @pl.when(n == 20 + u)

time: 86.2 us -> 85.6 us (level)
  no operation moved by 1% of the time
where the time goes in v5:
time: 85.6 us; the launch traced here: 85.5 us
  Pallas kernels  84.5 us (99%)
  local copies, waits for them, and re-layouts  0.97 us (1%)
    pallas_call x1, Pallas kernels, on_device(): pl.pallas_call(kernel, out_shape=pltpu.VMEM((ROWS, 1, SLOTS, ORDER, ORDER...  84.5 us

profile of v5, /device:TPU:1, one launch (start us, length us, event | category | flops | bytes accessed | tf_op | source)
XLA Modules:
  0.0 85.5 jit_solution(5001357222690152436)
XLA Ops:
  0.0 84.5 %shard_map.37 = f32[4,1,4,128,128]{4,3,2,1,0:T(8,128)S(1)} custom-call(f32[4,384,128]{2,1,0:T(8,128)} %bitcast.2, s32[3,1,4]{2,1,0:T(1,128)} %bitcast.3, s32[4,1,4]{2,1,0:T(1,128)} %rcols.1), custom_call_target="tpu_custom_call" | custom-call | tf_op jit(solution)/shard_map/pallas_call | solution.py:584
  84.5 1.0 %copy.5 = f32[4,1,4,128,128]{4,3,2,1,0:T(8,128)} copy(f32[4,1,4,128,128]{4,3,2,1,0:T(8,128)S(1)} %shard_map.37) | data formatting | bytes 2097152

commit v6 on v5

--- a/solution.py
+++ b/solution.py
@@ -129,27 +129,6 @@
     z_side = ((row, z_up * 2 + yl), (row, z_down * 2 + yl))
     alone = jnp.logical_and(yh == c, c == yl)
 
-    def unit_load(u, s):
-        p, part = lax.div(u, 2), lax.rem(u, 2)
-        rows = pl.ds(pl.multiple_of(s * ORDER + part * HALF, HALF), HALF)
-        return pltpu.make_async_copy(
-            vals.at[p, rows], abuf.at[z, u, s], unit_sem.at[u, s]
-        )
-
-    def row_load(p):
-        return pltpu.make_async_copy(
-            vals.at[p], stage.at[p, pl.ds(0, BODY)], stage_sem.at[p]
-        )
-
-    @pl.loop(0, UNITS)
-    def _(u):
-        for s in range(STORED):
-            unit_load(u, s).start()
-
-    @pl.loop(0, ROWS)
-    def _(p):
-        row_load(p).start()
-
     barrier = pltpu.get_barrier_semaphore()
 
     def greet(device):
@@ -166,6 +145,27 @@
         def _():
             greet((at_row(x, k, yh), z * 2 + c))
             greet((at_row(x, c, yl), z * 2 + k))
+
+    def unit_load(u, s):
+        p, part = lax.div(u, 2), lax.rem(u, 2)
+        rows = pl.ds(pl.multiple_of(s * ORDER + part * HALF, HALF), HALF)
+        return pltpu.make_async_copy(
+            vals.at[p, rows], abuf.at[z, u, s], unit_sem.at[u, s]
+        )
+
+    def row_load(p):
+        return pltpu.make_async_copy(
+            vals.at[p], stage.at[p, pl.ds(0, BODY)], stage_sem.at[p]
+        )
+
+    @pl.loop(0, UNITS)
+    def _(u):
+        for s in range(STORED):
+            unit_load(u, s).start()
+
+    @pl.loop(0, ROWS)
+    def _(p):
+        row_load(p).start()
 
     for p in range(ROWS):
         for s in range(8):

time: 85.6 us -> 85.5 us (level)
  no operation moved by 1% of the time
where the time goes in v6:
time: 85.5 us; the launch traced here: 85.4 us
  Pallas kernels  84.4 us (99%)
  local copies, waits for them, and re-layouts  0.97 us (1%)
    pallas_call x1, Pallas kernels, on_device(): pl.pallas_call(kernel, out_shape=pltpu.VMEM((ROWS, 1, SLOTS, ORDER, ORDER...  84.4 us

profile of v6, /device:TPU:1, one launch (start us, length us, event | category | flops | bytes accessed | tf_op | source)
XLA Modules:
  0.0 85.4 jit_solution(3621076203750199424)
XLA Ops:
  0.0 84.4 %shard_map.37 = f32[4,1,4,128,128]{4,3,2,1,0:T(8,128)S(1)} custom-call(f32[4,384,128]{2,1,0:T(8,128)} %bitcast.2, s32[3,1,4]{2,1,0:T(1,128)} %bitcast.3, s32[4,1,4]{2,1,0:T(1,128)} %rcols.1), custom_call_target="tpu_custom_call" | custom-call | tf_op jit(solution)/shard_map/pallas_call | solution.py:584
  84.4 1.0 %copy.5 = f32[4,1,4,128,128]{4,3,2,1,0:T(8,128)} copy(f32[4,1,4,128,128]{4,3,2,1,0:T(8,128)S(1)} %shard_map.37) | data formatting | bytes 2097152

commit v7 on v5

--- a/solution.py
+++ b/solution.py
@@ -56,7 +56,7 @@
     wanted += [(1, ROWS - 1, q, 2) for q in (0, 2)]
     rows = []
     for n in range(RING + 1):
-        room = 2 if n < RING else 4 * ROWS * ROWS
+        room = (0 if n == RING - 2 else 2) if n < RING else 4 * ROWS * ROWS
         for w in list(wanted):
             open_at = max(done[w[1]], *(ready.get((w[0], q), 0) for q in range(w[2], w[2] + w[3])))
             if open_at <= n and w[3] <= room:

time: 85.6 us -> 85.6 us (level)
  no operation moved by 1% of the time
where the time goes in v7:
time: 85.6 us; the launch traced here: 85.5 us
  Pallas kernels  84.5 us (99%)
  local copies, waits for them, and re-layouts  0.97 us (1%)
    pallas_call x1, Pallas kernels, on_device(): pl.pallas_call(kernel, out_shape=pltpu.VMEM((ROWS, 1, SLOTS, ORDER, ORDER...  84.5 us

profile of v7, /device:TPU:1, one launch (start us, length us, event | category | flops | bytes accessed | tf_op | source)
XLA Modules:
  0.0 85.5 jit_solution(12123087704744664175)
XLA Ops:
  0.0 84.5 %shard_map.37 = f32[4,1,4,128,128]{4,3,2,1,0:T(8,128)S(1)} custom-call(f32[4,384,128]{2,1,0:T(8,128)} %bitcast.2, s32[3,1,4]{2,1,0:T(1,128)} %bitcast.3, s32[4,1,4]{2,1,0:T(1,128)} %rcols.1), custom_call_target="tpu_custom_call" | custom-call | tf_op jit(solution)/shard_map/pallas_call | solution.py:584
  84.5 1.0 %copy.5 = f32[4,1,4,128,128]{4,3,2,1,0:T(8,128)} copy(f32[4,1,4,128,128]{4,3,2,1,0:T(8,128)S(1)} %shard_map.37) | data formatting | bytes 2097152
